TPU v7x, 128 devices: a whole 4x4x4 slice. The times are simulated.
128 devices in a mesh: ga: 4 (over y), dev: 32 (over x, z, core).
Axes of the slice: x: 4, y: 4, z: 4, core: 2. Of those that a mesh axis runs over, the one named last changes fastest.
Arguments:
- hidden_in: bfloat16 [1024, 2, 2048], P('dev'), may hold values from -6 to 6
- w_qkv: bfloat16 [2048, 4, 1280], P(None, 'ga'), may hold values from -0.125 to 0.125
- w_out: bfloat16 [4, 1024, 2048], P('ga'), may hold values from -0.09375 to 0.09375
- cache: bfloat16 [1024, 4, 2, 768, 128], P('dev', 'ga'), may hold values from -64 to 64, as said below
- lengths: int32 [1024], P('dev'), may hold values from 96 to 768, as said below
- w_router: bfloat16 [2048, 128], replicated, may hold values from -4 to 4
- routes: int32 [1024, 2, 8], P('dev'), may hold values from 0 to 127, all different within a row; in each aligned block of 64 rows (0 to 63, 64 to 127, ..., all dimensions but the last counted through in order) at most 10 rows name the same one
- w_gate_up: bfloat16 [128, 2048, 1536], P(('ga', 'dev')), may hold values from -0.125 to 0.125
- w_down: bfloat16 [128, 768, 2048], P(('ga', 'dev')), may hold values from -0.21875 to 0.21875
Outputs:
- layer_out: bfloat16 [1024, 2, 2048], P('dev', None, 'ga')
Inputs may be any that keep to these rules, and one draw needn't show every extreme that they name: Request r's cache holds lengths[r] live positions, 0 to lengths[r] - 1; its two new tokens stand at positions lengths[r] and lengths[r] + 1. Some request has exactly 768 and some exactly 96. `routes`: A row names 8 different experts. In each aligned block of 64 rows (the tokens of one index of dev, rows counted over requests and draft positions in order) no expert is named by more than 10 rows, a bound that some block reaches. `cache`: positions at or beyond a request's length hold data that is not part of its context.
All inputs are finite; a program needn't handle non-finite values.
Results may differ from a plain program's by a relative error of at most 0.01.
The roundings to bfloat16 on the way count: a program that leaves them out, or rounds other values in their place, can miss the bound.
Values may be sent and summed in bfloat16 or wider, within the bound.
A program may use at most 128 MiB of HBM per device.

v0:
```python
import jax
import jax.numpy as jnp
from jax import lax
from jax.sharding import PartitionSpec as P

ROPE_BASE = 1000000.0
NORM_EPS = 1e-06


def rotate_half(values, positions):
    half_width = values.shape[-1] // 2
    exponent = jnp.arange(half_width, dtype=jnp.float32) * (2.0 / values.shape[-1])
    angles = positions * ROPE_BASE ** (-exponent)
    cosine = jnp.cos(angles)
    sine_part = jnp.sin(angles)
    first_half = values[..., :half_width]
    second_half = values[..., half_width:]
    return jnp.concatenate(
        [
            first_half * cosine - second_half * sine_part,
            second_half * cosine + first_half * sine_part,
        ],
        axis=-1,
    )


def attend(normed, w_qkv, cache_rows, length_rows):
    head_dim = cache_rows.shape[-1]
    group_size = w_qkv.shape[2] // head_dim - 2
    projected = jnp.einsum("rtd,dkc->rtkc", normed, w_qkv, preferred_element_type=jnp.float32)
    req_count, draft_len, kv_local, unused_width = projected.shape
    positions = (length_rows[:, None] + jnp.arange(draft_len, dtype=jnp.int32)[None, :]).astype(
        jnp.float32
    )
    query_part = projected[..., : group_size * head_dim].reshape(
        req_count, draft_len, kv_local, group_size, head_dim
    )
    queries = rotate_half(query_part, positions[:, :, None, None, None]).astype(jnp.bfloat16)
    key_part = projected[..., group_size * head_dim : (group_size + 1) * head_dim]
    new_keys = rotate_half(key_part, positions[:, :, None, None]).astype(jnp.bfloat16)
    new_values = projected[..., (group_size + 1) * head_dim :].astype(jnp.bfloat16)
    score_scale = head_dim ** (-0.5)
    old_scores = (
        jnp.einsum(
            "rtkgh,rkch->rkgtc", queries, cache_rows[:, :, 0], preferred_element_type=jnp.float32
        )
        * score_scale
    )
    fresh_scores = (
        jnp.einsum("rtkgh,rskh->rkgts", queries, new_keys, preferred_element_type=jnp.float32)
        * score_scale
    )
    context = cache_rows.shape[3]
    old_live = jnp.arange(context, dtype=jnp.int32)[None, :] < length_rows[:, None]
    fresh_live = (
        jnp.arange(draft_len, dtype=jnp.int32)[None, :]
        <= jnp.arange(draft_len, dtype=jnp.int32)[:, None]
    )
    old_scores = jnp.where(old_live[:, None, None, None, :], old_scores, -jnp.inf)
    fresh_scores = jnp.where(fresh_live, fresh_scores, -jnp.inf)
    row_top = jnp.maximum(jnp.max(old_scores, axis=-1), jnp.max(fresh_scores, axis=-1))[..., None]
    old_exp = jnp.exp(old_scores - row_top)
    fresh_exp = jnp.exp(fresh_scores - row_top)
    totals = jnp.sum(old_exp, axis=-1) + jnp.sum(fresh_exp, axis=-1)
    mixed_sum = jnp.einsum(
        "rkgtc,rkch->rtkgh",
        old_exp.astype(jnp.bfloat16),
        cache_rows[:, :, 1],
        preferred_element_type=jnp.float32,
    )
    mixed_sum = mixed_sum + jnp.einsum(
        "rkgts,rskh->rtkgh",
        fresh_exp.astype(jnp.bfloat16),
        new_values,
        preferred_element_type=jnp.float32,
    )
    head_out = (mixed_sum / jnp.transpose(totals, (0, 3, 1, 2))[..., None]).astype(jnp.bfloat16)
    return head_out.reshape(req_count, draft_len, kv_local, group_size * head_dim)


def expert_rows(received, gate_up, down_proj, n_groups):
    quarter = received.shape[-1]
    ff_width = down_proj.shape[0]
    gate_up_split = gate_up.reshape(n_groups, quarter, 2 * ff_width)
    mixed_up = jnp.einsum(
        "gncq,gqf->ncf", received, gate_up_split, preferred_element_type=jnp.float32
    )
    activated = (jax.nn.silu(mixed_up[..., :ff_width]) * mixed_up[..., ff_width:]).astype(
        jnp.bfloat16
    )
    down_split = down_proj.reshape(ff_width, n_groups, quarter)
    produced = jnp.einsum(
        "ncf,fgq->gncq", activated, down_split, preferred_element_type=jnp.float32
    )
    return produced.astype(jnp.bfloat16)


def body(hidden_in, w_qkv, w_out, cache, lengths, w_router, routes, w_gate_up, w_down):
    n_groups = lax.axis_size("ga")
    n_members = lax.axis_size("dev")
    req_total, draft_len, model_width = hidden_in.shape
    experts = w_router.shape[1]
    top_count = routes.shape[2]
    quarter = model_width // n_groups
    group_index = lax.axis_index("ga")
    capacity = 2 * req_total * draft_len * top_count // experts + 2
    gate_up = w_gate_up[0]
    down_proj = w_down[0]
    req_count = hidden_in.shape[0]
    token_count = req_count * draft_len
    token_f32 = hidden_in.astype(jnp.float32)
    normed = (
        token_f32 * lax.rsqrt(jnp.mean(token_f32 * token_f32, axis=-1, keepdims=True) + NORM_EPS)
    ).astype(jnp.bfloat16)
    head_out = attend(normed, w_qkv, cache, lengths)
    partial_out = jnp.einsum("rtkf,kfd->rtd", head_out, w_out, preferred_element_type=jnp.float32)
    attn_cols = lax.psum_scatter(partial_out, "ga", scatter_dimension=2, tiled=True)
    own_cols = lax.dynamic_slice_in_dim(token_f32, group_index * quarter, quarter, 2)
    residual = (own_cols + attn_cols).astype(jnp.bfloat16)
    resid_f32 = residual.astype(jnp.float32)
    squares = lax.psum(jnp.sum(resid_f32 * resid_f32, axis=-1), "ga")
    mid_scale = lax.rsqrt(squares / model_width + NORM_EPS)
    normed_mid = (resid_f32 * mid_scale[..., None]).astype(jnp.bfloat16)
    flat_mid = normed_mid.reshape(token_count, quarter)
    router_rows = lax.dynamic_slice_in_dim(w_router, group_index * quarter, quarter, 0)
    logits = lax.psum(jnp.dot(flat_mid, router_rows, preferred_element_type=jnp.float32), "ga")
    flat_routes = routes.reshape(token_count, top_count)
    expert_ids = jnp.arange(experts, dtype=jnp.int32)
    picked = flat_routes[:, :, None] == expert_ids
    chosen = jnp.sum(jnp.where(picked, logits[:, None, :], 0.0), axis=-1)
    gates = jax.nn.softmax(chosen, axis=-1)
    gate_table = jnp.sum(jnp.where(picked, gates[:, :, None], 0.0), axis=1)
    hits = jnp.sum(picked.astype(jnp.int32), axis=1)
    slots = jnp.cumsum(hits, axis=0) - hits
    slot_ids = jnp.arange(capacity, dtype=jnp.int32)
    placed = (hits[:, :, None] == 1) & (slots[:, :, None] == slot_ids)
    selector = placed.astype(jnp.bfloat16)
    send_rows = jnp.einsum(
        "nec,nq->ecq", selector, flat_mid, preferred_element_type=jnp.float32
    ).astype(jnp.bfloat16)
    received = lax.all_to_all(send_rows, ("ga", "dev"), split_axis=0, concat_axis=0, tiled=True)
    slot_count = received.shape[1]
    grid_rows = received.reshape(n_groups, n_members, slot_count, quarter)
    produced = expert_rows(grid_rows, gate_up, down_proj, n_groups)
    returned = lax.all_to_all(
        produced.reshape(experts, slot_count, quarter),
        ("ga", "dev"),
        split_axis=0,
        concat_axis=0,
        tiled=True,
    )
    weight_table = jnp.where(placed, gate_table[:, :, None], 0.0)
    moe_sum = jnp.einsum(
        "nec,ecq->nq",
        weight_table,
        returned.astype(jnp.float32),
        precision=lax.Precision.HIGHEST,
        preferred_element_type=jnp.float32,
    )
    return (resid_f32 + moe_sum.reshape(resid_f32.shape)).astype(jnp.bfloat16)


def solution(mesh):
    return jax.shard_map(
        body,
        mesh=mesh,
        in_specs=(
            P("dev", None, None),
            P(None, "ga", None),
            P("ga", None, None),
            P("dev", "ga", None, None, None),
            P("dev"),
            P(),
            P("dev", None, None),
            P(("ga", "dev"), None, None),
            P(("ga", "dev"), None, None),
        ),
        out_specs=P("dev", None, "ga"),
        check_vma=False,
    )
```

profile of v0, /device:TPU:4, one launch (start us, length us, event | category | flops | bytes accessed | tf_op | source)
XLA Modules:
  0.0 159.7 jit_solution(7217690667684907534)
XLA Ops:
  6.6 0.7 add_convert_fusion.2
  7.3 0.7 iota_compare_fusion.2
  8.0 1.1 multiply_reduce_fusion
  9.1 3.7 %fusion.13 = f32[32,2,1,1280]{3,0,1,2:T(8,128)S(1)} fusion(bf16[2048,1,1280]{2,0,1:T(8,128)(2,1)} %param.10, f32[32,2]{0,1:T(2,128)S(1)} %add_rsqrt_fusion.1, bf16[32,2,2048]{2,1,0:T(2,128)(2,1)} %param.9), kind=kOutput, calls=%fused_computation.14 | convolution fusion | flops 335937536 | bytes 5832960 | tf_op jit(solution)/shard_map/rtd,dkc->rtkc/dot_general | solution.py:30
  14.1 0.8 fusion.89
  14.8 5.2 %fusion.88 = (f32[32,8,2]{1,2,0:T(2,128)S(1)}, f32[32,1,8,2,768]{4,2,3,0,1:T(8,128)S(1)}) fusion(bf16[32,1,2,768,128]{4,3,2,1,0:T(8,128)(2,1)} %param.12, bf16[32,2,8,64]{3,2,1,0:T(8,128)(2,1)S(1)} %get-tuple-element.8, bf16[32,2,8,64]{3,2,1,0:T(8,128)(2,1)S(1)} %get-tuple-element.7, pred[32,768]{1,0:T(8,128)(4,1)S(1)} %iota_compare_fusion.2), kind=kOutput, calls=%fused_computation.111 | convolution fusion | flops 102104576 | bytes 8022016 | tf_op jit(solution)/shard_map/rtkgh,rkch->rkgtc/dot_general | solution.py:44
  20.5 1.0 fusion.26
  22.0 3.9 %fusion.8 = f32[32,2,2048]{2,0,1:T(8,128)} fusion(bf16[1,1024,2048]{2,1,0:T(8,128)(2,1)} %param.11, bf16[32,2,1024]{2,1,0:T(2,128)(2,1)S(1)} %reshape.288), kind=kOutput, calls=%fused_computation.8 | convolution fusion | flops 268435456 | bytes 4849664 | tf_op jit(solution)/shard_map/rtkf,kfd->rtd/dot_general | solution.py:116
  26.4 23.4 %reduce-scatter.2.cloned.1.call-done = f32[32,2,512]{2,0,1:T(8,128)} async-done(((f32[32,2,2048]{2,0,1:T(8,128)}), f32[32,2,512]{2,0,1:T(8,128)}) %reduce-scatter.2.cloned.1.call-update) | async-done | bytes 131088 | tf_op jit(solution)/shard_map/reduce_scatter | solution.py:117
  49.9 1.0 fusion.54
  50.9 8.3 %psum.14 = f32[32,2]{0,1:T(2,128)S(1)} all-reduce(f32[32,2]{0,1:T(2,128)S(1)} %get-tuple-element.5), channel_id=1, replica_groups=mesh['ga'=4,'dev'=32] {'ga'}, use_global_device_ids=true, to_apply=%region_9.10 | all-reduce | flops 64 | bytes 512 | tf_op jit(solution)/shard_map/psum | solution.py:121
  59.4 0.6 convolution_convert_fusion
  60.0 2.2 %copy.87 = bf16[128,10,512]{2,1,0:T(8,128)(2,1)} copy(bf16[128,10,512]{2,0,1:T(8,128)(2,1)S(1)} %convolution_convert_fusion) | data formatting | bytes 2621440 | tf_op jit(solution)/shard_map/convert_element_type | solution.py:140
  62.2 7.8 %all-to-all-start = ((bf16[128,10,512]{2,1,0:T(8,128)(2,1)}), bf16[128,10,512]{2,1,0:T(8,128)(2,1)S(1)}, u32[]{:S(2)}, u32[]{:S(2)}) async-start(bf16[128,10,512]{2,1,0:T(8,128)(2,1)} %copy.87), calls=%async_computation.1 | async-start | bytes 4194304 | tf_op jit(solution)/shard_map/all_to_all | solution.py:141
  70.0 6.2 %reshape_squeeze.7 = bf16[768,4,512]{2,1,0:T(4,128)(2,1)} reshape(bf16[1,768,2048]{2,1,0:T(8,128)(2,1)} %param.17) | data formatting | bytes 6291456 | tf_op jit(solution)/shard_map/reshape;squeeze | solution.py:91
  76.2 22.3 %all-to-all-done = bf16[128,10,512]{2,1,0:T(8,128)(2,1)S(1)} async-done(((bf16[128,10,512]{2,1,0:T(8,128)(2,1)}), bf16[128,10,512]{2,1,0:T(8,128)(2,1)S(1)}, u32[]{:S(2)}, u32[]{:S(2)}) %all-to-all-start) | async-done | bytes 1310752 | tf_op jit(solution)/shard_map/all_to_all | solution.py:141
  98.5 0.7 copy.88
  99.2 5.1 %convolution_bitcast_fusion = f32[32,10,1536]{2,0,1:T(8,128)S(1)} fusion(bf16[4,32,10,512]{3,1,0,2:T(8,128)(2,1)S(1)} %bitcast.126, bf16[4,512,1536,1]{2,1,0,3:T(8,128)(2,1)} %bitcast.131), kind=kOutput, calls=%fused_computation.13 | convolution fusion | flops 2013265920 | bytes 9568256 | tf_op jit(solution)/shard_map/gncq,gqf->ncf/dot_general | solution.py:85
  104.4 1.6 %fusion.16 = bf16[32,10,4,512]{3,0,2,1:T(8,128)(2,1)S(1)} fusion(bf16[768,4,512]{2,1,0:T(4,128)(2,1)S(1)} %copy-done.2, f32[32,10,1536]{2,0,1:T(8,128)S(1)} %convolution_bitcast_fusion), kind=kOutput, calls=%fused_computation.15 | convolution fusion | flops 1008762880 | bytes 6422528 | tf_op jit(solution)/shard_map/ncf,fgq->gncq/dot_general | solution.py:92
  106.0 2.2 %copy.90 = bf16[128,10,512]{2,1,0:T(8,128)(2,1)} copy(bf16[128,10,512]{2,0,1:T(8,128)(2,1)S(1)} %bitcast.125) | data formatting | bytes 2621440 | tf_op jit(solution)/shard_map/reshape | solution.py:146
  108.2 6.5 %all-to-all-start.1 = ((bf16[128,10,512]{2,1,0:T(8,128)(2,1)}), bf16[128,10,512]{2,1,0:T(8,128)(2,1)S(1)}, u32[]{:S(2)}, u32[]{:S(2)}) async-start(bf16[128,10,512]{2,1,0:T(8,128)(2,1)} %copy.90), calls=%async_computation.2 | async-start | bytes 4194304 | tf_op jit(solution)/shard_map/all_to_all | solution.py:145
  114.9 34.3 %psum.15 = f32[64,128]{1,0:T(8,128)S(1)} all-reduce(f32[64,128]{1,0:T(8,128)S(1)} %fusion.60), channel_id=1, replica_groups=mesh['ga'=4,'dev'=32] {'ga'}, use_global_device_ids=true, to_apply=%region_10.11 | all-reduce | flops 8192 | bytes 65536 | tf_op jit(solution)/shard_map/psum | solution.py:126
  150.0 2.1 %fusion.30 = f32[64,512]{1,0:T(8,128)S(1)} fusion(bf16[128,10,512]{2,1,0:T(8,128)(2,1)S(1)} %all-to-all-done.1, f32[64,128]{1,0:T(8,128)S(1)} %select_reduce_fusion, s32[64,128]{1,0:T(8,128)S(1)} %sub.47, pred[64,128]{1,0:T(8,128)(4,1)S(1)} %broadcast_compare_fusion), kind=kOutput, calls=%fused_computation.27 | convolution fusion | flops 503562240 | bytes 1515520 | tf_op jit(solution)/shard_map/nec,ecq->nq/dot_general | solution.py:153
  152.2 0.7 copy.93
  (52 shorter events, 3.9 us)
Async XLA Ops:
  6.5 108.2 %copy-start = (bf16[2048,128]{1,0:T(8,128)(2,1)S(1)}, bf16[2048,128]{1,0:T(8,128)(2,1)}, u32[]{:S(2)}) copy-start(bf16[2048,128]{1,0:T(8,128)(2,1)} %param.14) | copy-start | bytes 1572868
  6.5 43.3 %reduce-scatter.2.cloned.1.call-start = ((), (), s32[]{:S(2)}) async-start(), calls=%async_computation.3 | async-start | bytes 655360 | tf_op jit(solution)/shard_map/reduce_scatter | solution.py:117
  13.7 6.8 %copy-start.1 = (bf16[32,1,2,768,128]{4,3,2,1,0:T(8,128)(2,1)S(1)}, bf16[32,1,2,768,128]{4,3,2,1,0:T(8,128)(2,1)}, u32[]{:S(2)}) copy-start(bf16[32,1,2,768,128]{4,3,2,1,0:T(8,128)(2,1)} %param.12) | copy-start | bytes 37748740
  22.0 3.9 %copy-start.4 = (s32[32,2,8]{0,2,1:T(8,128)S(1)}, s32[32,2,8]{0,2,1:T(8,128)}, u32[]{:S(2)}) copy-start(s32[32,2,8]{0,2,1:T(8,128)} %param.15) | copy-start | bytes 6148
  22.0 4.3 %copy-start.3 = (bf16[32,2,2048]{2,1,0:T(2,128)(2,1)S(1)}, bf16[32,2,2048]{2,1,0:T(2,128)(2,1)}, u32[]{:S(2)}) copy-start(bf16[32,2,2048]{2,1,0:T(2,128)(2,1)} %param.9) | copy-start | bytes 786436
  62.2 36.3 %all-to-all-start = ((bf16[128,10,512]{2,1,0:T(8,128)(2,1)}), bf16[128,10,512]{2,1,0:T(8,128)(2,1)S(1)}, u32[]{:S(2)}, u32[]{:S(2)}) async-start(bf16[128,10,512]{2,1,0:T(8,128)(2,1)} %copy.87), calls=%async_computation.1 | async-start | bytes 4194304 | tf_op jit(solution)/shard_map/all_to_all | solution.py:141
  99.2 5.1 %copy-start.2 = (bf16[768,4,512]{2,1,0:T(4,128)(2,1)S(1)}, bf16[768,4,512]{2,1,0:T(4,128)(2,1)}, u32[]{:S(2)}) copy-start(bf16[768,4,512]{2,1,0:T(4,128)(2,1)} %reshape_squeeze.7) | copy-start | bytes 9437188
  108.2 41.8 %all-to-all-start.1 = ((bf16[128,10,512]{2,1,0:T(8,128)(2,1)}), bf16[128,10,512]{2,1,0:T(8,128)(2,1)S(1)}, u32[]{:S(2)}, u32[]{:S(2)}) async-start(bf16[128,10,512]{2,1,0:T(8,128)(2,1)} %copy.90), calls=%async_computation.2 | async-start | bytes 4194304 | tf_op jit(solution)/shard_map/all_to_all | solution.py:145
Sparse Core Ops, SparseCore 0:
  26.1 23.7 reduce-scatter.1
where the time goes:
time: 160 us
  waiting for transfers between devices  45.8 us (29%)
  blocking collectives  42.6 us (27%)
  matrix products  24.3 us (15%)
  starting transfers between devices  14.3 us (9%)
  between operations  13.7 us (9%)
  local copies, waits for them, and re-layouts  12.7 us (8%)
  other arithmetic  6.19 us (4%)
    psum x1, blocking collectives, body(): lax.psum(jnp.dot(flat_mid, router_rows, preferred_element_type=jnp.float3...  34.3 us
    reduce_scatter x1, waiting for transfers between devices, body(): lax.psum_scatter(partial_out, 'ga', scatter_dimension=2, tiled=True)  23.4 us
    all_to_all x1, waiting for transfers between devices, body(): lax.all_to_all(send_rows, ('ga', 'dev'), split_axis=0, concat_axis=0, til...  22.3 us
    psum x1, blocking collectives, body(): squares = lax.psum(jnp.sum(resid_f32 * resid_f32, axis=-1), 'ga')  8.34 us
    all_to_all x1, starting transfers between devices, body(): lax.all_to_all(send_rows, ('ga', 'dev'), split_axis=0, concat_axis=0, til...  7.84 us
    all_to_all x1, starting transfers between devices, body(): lax.all_to_all(produced.reshape(experts, slot_count, quarter), ('ga', 'de...  6.5 us
    another operation x1, local copies, waits for them, and re-layouts, expert_rows(): down_split = down_proj.reshape(ff_width, n_groups, quarter)  6.16 us
    dot_general x1, matrix products, attend(): jnp.einsum('rtkgh,rkch->rkgtc', queries, cache_rows[:, :, 0], preferred_e...  5.16 us
  transfers between devices with their start and end apart: 3, of which 2 were waited for; matrix products, arithmetic and copies ran while one was open for 5% of the time, Pallas kernels for 0%

commit v1 on v0

v1 whole, which is shorter than its diff:
```python
import jax
import jax.numpy as jnp
from jax import lax
from jax.experimental import pallas as pl
from jax.experimental.pallas import tpu as pltpu
from jax.sharding import PartitionSpec as P

ROPE_BASE = 1000000.0
NORM_EPS = 1e-06


def rotate_half(values, positions):
    half_width = values.shape[-1] // 2
    exponent = jnp.arange(half_width, dtype=jnp.float32) * (2.0 / values.shape[-1])
    angles = positions * ROPE_BASE ** (-exponent)
    cosine = jnp.cos(angles)
    sine_part = jnp.sin(angles)
    first_half = values[..., :half_width]
    second_half = values[..., half_width:]
    return jnp.concatenate(
        [
            first_half * cosine - second_half * sine_part,
            second_half * cosine + first_half * sine_part,
        ],
        axis=-1,
    )


def attend(normed, w_qkv, cache_rows, length_rows):
    head_dim = cache_rows.shape[-1]
    group_size = w_qkv.shape[2] // head_dim - 2
    projected = jnp.einsum("rtd,dkc->rtkc", normed, w_qkv, preferred_element_type=jnp.float32)
    req_count, draft_len, kv_local, unused_width = projected.shape
    positions = (length_rows[:, None] + jnp.arange(draft_len, dtype=jnp.int32)[None, :]).astype(
        jnp.float32
    )
    query_part = projected[..., : group_size * head_dim].reshape(
        req_count, draft_len, kv_local, group_size, head_dim
    )
    queries = rotate_half(query_part, positions[:, :, None, None, None]).astype(jnp.bfloat16)
    key_part = projected[..., group_size * head_dim : (group_size + 1) * head_dim]
    new_keys = rotate_half(key_part, positions[:, :, None, None]).astype(jnp.bfloat16)
    new_values = projected[..., (group_size + 1) * head_dim :].astype(jnp.bfloat16)
    score_scale = head_dim ** (-0.5)
    old_scores = (
        jnp.einsum(
            "rtkgh,rkch->rkgtc", queries, cache_rows[:, :, 0], preferred_element_type=jnp.float32
        )
        * score_scale
    )
    fresh_scores = (
        jnp.einsum("rtkgh,rskh->rkgts", queries, new_keys, preferred_element_type=jnp.float32)
        * score_scale
    )
    context = cache_rows.shape[3]
    old_live = jnp.arange(context, dtype=jnp.int32)[None, :] < length_rows[:, None]
    fresh_live = (
        jnp.arange(draft_len, dtype=jnp.int32)[None, :]
        <= jnp.arange(draft_len, dtype=jnp.int32)[:, None]
    )
    old_scores = jnp.where(old_live[:, None, None, None, :], old_scores, -jnp.inf)
    fresh_scores = jnp.where(fresh_live, fresh_scores, -jnp.inf)
    row_top = jnp.maximum(jnp.max(old_scores, axis=-1), jnp.max(fresh_scores, axis=-1))[..., None]
    old_exp = jnp.exp(old_scores - row_top)
    fresh_exp = jnp.exp(fresh_scores - row_top)
    totals = jnp.sum(old_exp, axis=-1) + jnp.sum(fresh_exp, axis=-1)
    mixed_sum = jnp.einsum(
        "rkgtc,rkch->rtkgh",
        old_exp.astype(jnp.bfloat16),
        cache_rows[:, :, 1],
        preferred_element_type=jnp.float32,
    )
    mixed_sum = mixed_sum + jnp.einsum(
        "rkgts,rskh->rtkgh",
        fresh_exp.astype(jnp.bfloat16),
        new_values,
        preferred_element_type=jnp.float32,
    )
    head_out = (mixed_sum / jnp.transpose(totals, (0, 3, 1, 2))[..., None]).astype(jnp.bfloat16)
    return head_out.reshape(req_count, draft_len, kv_local, group_size * head_dim)


N_GROUPS = 4
N_MEMBERS = 32
TOKENS = 64
WIDTH = 2048
QUARTER = 512
FF = 768
EXPERTS = 128
ROWS = 16 * N_MEMBERS
PACKED = 1280
F32 = jnp.float32
BF16 = jnp.bfloat16


def iota(shape, axis):
    return lax.broadcasted_iota(jnp.int32, shape, axis)


def dot(a, b):
    return jnp.dot(a, b, preferred_element_type=F32)


def dot_nt(a, b):
    return lax.dot_general(a, b, (((1,), (1,)), ((), ())), preferred_element_type=F32)


def one_hot(mask):
    return jnp.where(mask, 1.0, 0.0).astype(BF16)


def layer_kernel(
    heads_ref,
    hidden_ref,
    router_ref,
    routes_ref,
    w_out_hbm,
    gate_up_hbm,
    down_hbm,
    out_ref,
    w_out,
    gate_up,
    down,
    part_out,
    part_in,
    resid,
    mid,
    sel_a,
    sel_b,
    comb_a,
    comb_b,
    send,
    recv,
    back,
    home,
    rows,
    acts,
    made,
    moe_out,
    moe_in,
    load_sem,
    rs_sem,
    ag_sem,
    go_send,
    go_recv,
    back_send,
    back_recv,
    fin_sem,
):
    group = lax.axis_index("ga")
    member = lax.axis_index("dev")

    def peer(offset):
        return lax.rem(group + offset, N_GROUPS)

    def other(offset):
        return lax.rem(member + offset, N_MEMBERS)

    order = (2, 1, 3, 0)
    loads = {}
    for offset in order:
        columns = pl.ds(pl.multiple_of(peer(offset) * QUARTER, QUARTER), QUARTER)
        loads[offset] = pltpu.make_async_copy(
            w_out_hbm.at[:, columns], w_out.at[offset], load_sem.at[offset]
        )
        loads[offset].start()
    load_gate_up = pltpu.make_async_copy(gate_up_hbm, gate_up, load_sem.at[4])
    load_gate_up.start()
    load_down = pltpu.make_async_copy(down_hbm, down, load_sem.at[5])
    load_down.start()

    barrier = pltpu.get_barrier_semaphore()
    for offset in range(1, N_GROUPS):
        pl.semaphore_signal(
            barrier,
            inc=1,
            device_id={"ga": peer(offset)},
            device_id_type=pl.DeviceIdType.MESH,
        )

    @pl.loop(1, N_MEMBERS)
    def _(offset):
        pl.semaphore_signal(
            barrier,
            inc=1,
            device_id={"dev": other(offset)},
            device_id_type=pl.DeviceIdType.MESH,
        )

    heads = heads_ref[...]
    parts = {}
    for place, offset in enumerate(order):
        loads[offset].wait()
        part_out[offset] = dot(heads, w_out[offset])
        if place == 0:
            pl.semaphore_wait(barrier, N_GROUPS - 1 + N_MEMBERS - 1)
        if offset:
            parts[offset] = pltpu.make_async_remote_copy(
                src_ref=part_out.at[offset],
                dst_ref=part_in.at[offset],
                send_sem=rs_sem.at[0, offset],
                recv_sem=rs_sem.at[1, offset],
                device_id={"ga": peer(offset)},
                device_id_type=pl.DeviceIdType.MESH,
            )
            parts[offset].start()

    expert_of = iota((TOKENS, EXPERTS), 1)
    routes = routes_ref[...]
    hit = routes[:, 0:1] == expert_of
    for choice in range(1, routes.shape[1]):
        hit = hit | (routes[:, choice : choice + 1] == expert_of)
    earlier = one_hot(iota((TOKENS, TOKENS), 0) > iota((TOKENS, TOKENS), 1))
    slots = dot(earlier, one_hot(hit))
    code = jnp.where(hit, slots, -1.0).astype(BF16)
    code_a = jnp.concatenate([code] * 2, axis=0)
    code_b = jnp.concatenate([code] * 8, axis=0)
    first = group * N_MEMBERS
    spread = one_hot(iota((ROWS, EXPERTS), 0) // 16 + first == iota((ROWS, EXPERTS), 1))
    gather = one_hot(iota((EXPERTS, ROWS), 1) // 16 + first == iota((EXPERTS, ROWS), 0))

    row, col = iota((ROWS, 2 * TOKENS), 0), iota((ROWS, 2 * TOKENS), 1)
    sel_a[...] = one_hot(
        (dot_nt(spread, code_a) == (row % 8).astype(F32)) & ((row // 8) % 2 == col // TOKENS)
    )
    row, col = iota((ROWS, 8 * TOKENS), 0), iota((ROWS, 8 * TOKENS), 1)
    sel_b[...] = one_hot(
        (dot_nt(spread, code_b) == (8 + row % 2).astype(F32)) & ((row // 2) % 8 == col // TOKENS)
    )
    row, col = iota((2 * TOKENS, ROWS), 0), iota((2 * TOKENS, ROWS), 1)
    mask_a = (dot(code_a, gather) == (col % 8).astype(F32)) & ((col // 8) % 2 == row // TOKENS)
    row, col = iota((8 * TOKENS, ROWS), 0), iota((8 * TOKENS, ROWS), 1)
    mask_b = (dot(code_b, gather) == (8 + col % 2).astype(F32)) & ((col // 2) % 8 == row // TOKENS)

    for offset in (1, 3, 2):
        parts[offset].wait()
    attn = part_out[0] + part_in[1] + part_in[2] + part_in[3]
    own = pl.ds(pl.multiple_of(group * QUARTER, QUARTER), QUARTER)
    resid[group] = (hidden_ref[:, own].astype(F32) + attn).astype(BF16)
    quarters = {}
    for offset in (2, 1, 3):
        quarters[offset] = pltpu.make_async_remote_copy(
            src_ref=resid.at[group],
            dst_ref=resid.at[group],
            send_sem=ag_sem.at[0, offset],
            recv_sem=ag_sem.at[1, offset],
            device_id={"ga": peer(offset)},
            device_id_type=pl.DeviceIdType.MESH,
        )
        quarters[offset].start()
    for offset in (1, 3, 2):
        quarters[offset].wait_send()
        pltpu.make_async_remote_copy(
            src_ref=resid.at[group],
            dst_ref=resid.at[peer(N_GROUPS - offset)],
            send_sem=ag_sem.at[0, offset],
            recv_sem=ag_sem.at[1, offset],
            device_id={"ga": peer(offset)},
            device_id_type=pl.DeviceIdType.MESH,
        ).wait_recv()

    squares = jnp.zeros((TOKENS, 1), F32)
    for quarter in range(N_GROUPS):
        values = resid[quarter].astype(F32)
        squares = squares + jnp.sum(values * values, axis=-1, keepdims=True)
    scale = lax.rsqrt(squares / WIDTH + NORM_EPS)
    for quarter in range(N_GROUPS):
        mid[:, quarter * QUARTER : (quarter + 1) * QUARTER] = (
            resid[quarter].astype(F32) * scale
        ).astype(BF16)

    stacked = jnp.concatenate([mid[:, :1024], mid[:, 1024:]], axis=0)
    packed_a = dot(sel_a[...], stacked).astype(BF16)
    send[:, :, :1024] = packed_a.reshape(N_MEMBERS, 16, 1024)
    stacked = jnp.concatenate([mid[:, 256 * k : 256 * k + 256] for k in range(8)], axis=0)
    packed_b = dot(sel_b[...], stacked).astype(BF16)
    send[:, :, 1024:] = packed_b.reshape(N_MEMBERS, 16, 256)

    def going(offset):
        return pltpu.make_async_remote_copy(
            src_ref=send.at[other(offset)],
            dst_ref=recv.at[member],
            send_sem=go_send.at[offset],
            recv_sem=go_recv.at[offset],
            device_id={"dev": other(offset)},
            device_id_type=pl.DeviceIdType.MESH,
        )

    @pl.loop(1, N_MEMBERS)
    def _(offset):
        going(offset).start()

    recv[member] = send[member]

    logits = dot(mid[...], router_ref[...])
    top = jnp.max(jnp.where(hit, logits, -jnp.inf), axis=-1, keepdims=True)
    raised = jnp.where(hit, jnp.exp(logits - top), 0.0)
    gates = raised / jnp.sum(raised, axis=-1, keepdims=True)
    rest = gates
    for term in range(3):
        piece = rest.astype(BF16)
        rest = rest - piece.astype(F32)
        spread_a = dot(jnp.concatenate([piece] * 2, axis=0), gather)
        comb = jnp.where(mask_a, spread_a, 0.0).astype(BF16)
        for half in range(2):
            comb_a[half, term * TOKENS : (term + 1) * TOKENS] = comb[
                half * TOKENS : (half + 1) * TOKENS
            ]
        spread_b = dot(jnp.concatenate([piece] * 8, axis=0), gather)
        comb = jnp.where(mask_b, spread_b, 0.0).astype(BF16)
        for eighth in range(8):
            comb_b[eighth, term * TOKENS : (term + 1) * TOKENS] = comb[
                eighth * TOKENS : (eighth + 1) * TOKENS
            ]

    load_gate_up.wait()
    load_down.wait()

    @pl.loop(1, N_MEMBERS)
    def _(offset):
        going(offset).wait_send()
        pltpu.make_async_remote_copy(
            src_ref=send.at[other(offset)],
            dst_ref=recv.at[other(N_MEMBERS - offset)],
            send_sem=go_send.at[offset],
            recv_sem=go_recv.at[offset],
            device_id={"dev": other(offset)},
            device_id_type=pl.DeviceIdType.MESH,
        ).wait_recv()

    row, col = iota((ROWS, ROWS), 0), iota((ROWS, ROWS), 1)
    unpack = one_hot(((row % 64) // 2) * 16 + (row // 64) * 2 + row % 2 == col)
    pack = one_hot(((col % 64) // 2) * 16 + (col // 64) * 2 + col % 2 == row)
    got = recv[:, :, :1024].astype(F32)
    for half in range(2):
        rows[:256, half * 1024 : (half + 1) * 1024] = (
            got[:, half * 8 : half * 8 + 8].reshape(256, 1024).astype(BF16)
        )
    sorted_b = dot(unpack, recv[:, :, 1024:].reshape(ROWS, 256)).astype(BF16)
    for k in range(8):
        rows[256:, 256 * k : 256 * k + 256] = sorted_b[64 * k : 64 * k + 64]
    for chunk in range(3):
        columns = slice(256 * chunk, 256 * chunk + 256)
        gate = dot(rows[...], gate_up[:, columns])
        up = dot(rows[...], gate_up[:, FF + 256 * chunk : FF + 256 * chunk + 256])
        acts[:, columns] = (gate / (1.0 + jnp.exp(-gate)) * up).astype(BF16)
    for chunk in range(8):
        result = dot(acts[...], down[:, 256 * chunk : 256 * chunk + 256])
        half, place = chunk // 4, (chunk % 4) * 256
        back[:, half * 8 : half * 8 + 8, place : place + 256] = result[:256].reshape(
            N_MEMBERS, 8, 256
        ).astype(BF16)
        made[64 * chunk : 64 * chunk + 64] = result[256:].astype(BF16)
    back[:, :, 1024:] = dot(pack, made[...]).astype(BF16).reshape(N_MEMBERS, 16, 256)

    def returning(offset):
        return pltpu.make_async_remote_copy(
            src_ref=back.at[other(offset)],
            dst_ref=home.at[member],
            send_sem=back_send.at[offset],
            recv_sem=back_recv.at[offset],
            device_id={"dev": other(offset)},
            device_id_type=pl.DeviceIdType.MESH,
        )

    @pl.loop(1, N_MEMBERS)
    def _(offset):
        returning(offset).start()

    home[member] = back[member]

    @pl.loop(1, N_MEMBERS)
    def _(offset):
        returning(offset).wait_send()
        pltpu.make_async_remote_copy(
            src_ref=back.at[other(offset)],
            dst_ref=home.at[other(N_MEMBERS - offset)],
            send_sem=back_send.at[offset],
            recv_sem=back_recv.at[offset],
            device_id={"dev": other(offset)},
            device_id_type=pl.DeviceIdType.MESH,
        ).wait_recv()

    finals = {}
    for offset in order:
        quarter = peer(offset)
        place = pl.ds(pl.multiple_of((quarter % 2) * QUARTER, QUARTER), QUARTER)
        summed = dot(comb_a[quarter // 2], home[:, :, place].reshape(ROWS, QUARTER))
        summed = summed[:TOKENS] + summed[TOKENS : 2 * TOKENS] + summed[2 * TOKENS :]
        moe_out[offset] = summed
        last = home[:, :, 1024:].reshape(ROWS, 256)
        for k in range(2):
            more = dot(comb_b[2 * quarter + k], last)
            more = more[:TOKENS] + more[TOKENS : 2 * TOKENS] + more[2 * TOKENS :]
            moe_out[offset, :, 256 * k : 256 * k + 256] += more
        if offset:
            finals[offset] = pltpu.make_async_remote_copy(
                src_ref=moe_out.at[offset],
                dst_ref=moe_in.at[offset],
                send_sem=fin_sem.at[0, offset],
                recv_sem=fin_sem.at[1, offset],
                device_id={"ga": peer(offset)},
                device_id_type=pl.DeviceIdType.MESH,
            )
            finals[offset].start()
    for offset in (1, 3, 2):
        finals[offset].wait()
    moe = moe_out[0] + moe_in[1] + moe_in[2] + moe_in[3]
    out_ref[...] = (resid[group].astype(F32) + moe).astype(BF16)


def layer(heads, hidden, w_router, routes, w_out, gate_up, down):
    vmem = pl.BlockSpec(memory_space=pltpu.VMEM)
    hbm = pl.BlockSpec(memory_space=pl.ANY)
    dma = pltpu.SemaphoreType.DMA
    packed = pltpu.VMEM((N_MEMBERS, 16, PACKED), BF16)
    parts = pltpu.VMEM((N_GROUPS, TOKENS, QUARTER), F32)
    return pl.pallas_call(
        layer_kernel,
        out_shape=jax.ShapeDtypeStruct((TOKENS, QUARTER), BF16),
        in_specs=[vmem] * 4 + [hbm] * 3,
        out_specs=vmem,
        scratch_shapes=[
            pltpu.VMEM((N_GROUPS, 1024, QUARTER), BF16),
            pltpu.VMEM((WIDTH, 2 * FF), BF16),
            pltpu.VMEM((FF, WIDTH), BF16),
            parts,
            parts,
            pltpu.VMEM((N_GROUPS, TOKENS, QUARTER), BF16),
            pltpu.VMEM((TOKENS, WIDTH), BF16),
            pltpu.VMEM((ROWS, 2 * TOKENS), BF16),
            pltpu.VMEM((ROWS, 8 * TOKENS), BF16),
            pltpu.VMEM((2, 3 * TOKENS, ROWS), BF16),
            pltpu.VMEM((8, 3 * TOKENS, ROWS), BF16),
            packed,
            packed,
            packed,
            packed,
            pltpu.VMEM((320, WIDTH), BF16),
            pltpu.VMEM((320, FF), BF16),
            pltpu.VMEM((ROWS, 256), BF16),
            parts,
            parts,
            dma((6,)),
            dma((2, N_GROUPS)),
            dma((2, N_GROUPS)),
            dma((N_MEMBERS,)),
            dma((N_MEMBERS,)),
            dma((N_MEMBERS,)),
            dma((N_MEMBERS,)),
            dma((2, N_GROUPS)),
        ],
        compiler_params=pltpu.CompilerParams(
            collective_id=0, has_side_effects=True, vmem_limit_bytes=48 * 1024 * 1024
        ),
    )(heads, hidden, w_router, routes, w_out, gate_up, down)


def body(hidden_in, w_qkv, w_out, cache, lengths, w_router, routes, w_gate_up, w_down):
    req_count, draft_len, model_width = hidden_in.shape
    token_f32 = hidden_in.astype(jnp.float32)
    normed = (
        token_f32 * lax.rsqrt(jnp.mean(token_f32 * token_f32, axis=-1, keepdims=True) + NORM_EPS)
    ).astype(jnp.bfloat16)
    head_out = attend(normed, w_qkv, cache, lengths)
    out = layer(
        head_out.reshape(TOKENS, 1024),
        hidden_in.reshape(TOKENS, model_width),
        w_router,
        routes.reshape(TOKENS, 8),
        w_out[0],
        w_gate_up[0],
        w_down[0],
    )
    return out.reshape(req_count, draft_len, QUARTER)


def solution(mesh):
    return jax.shard_map(
        body,
        mesh=mesh,
        in_specs=(
            P("dev", None, None),
            P(None, "ga", None),
            P("ga", None, None),
            P("dev", "ga", None, None, None),
            P("dev"),
            P(),
            P("dev", None, None),
            P(("ga", "dev"), None, None),
            P(("ga", "dev"), None, None),
        ),
        out_specs=P("dev", None, "ga"),
        check_vma=False,
    )
```

time: 160 us -> 96.1 us (0.60)
  the two profiles are of different devices: /device:TPU:4 before, /device:TPU:1 now
where the time goes in v1:
time: 96.1 us; the launch traced here: 95.2 us
  Pallas kernels  74.4 us (77%)
  matrix products  13.3 us (14%)
  other arithmetic  5.47 us (6%)
  local copies, waits for them, and re-layouts  1.87 us (2%)
    pallas_call x1, Pallas kernels, layer(): pl.pallas_call(layer_kernel, out_shape=jax.ShapeDtypeStruct((TOKENS, QUAR...  74.4 us
    dot_general x1, matrix products, attend(): jnp.einsum('rtkgh,rkch->rkgtc', queries, cache_rows[:, :, 0], preferred_e...  4.68 us
    dot_general x1, matrix products, attend(): jnp.einsum('rkgtc,rkch->rtkgh', old_exp.astype(jnp.bfloat16), cache_rows[...  3.99 us
    dot_general x1, matrix products, attend(): jnp.einsum('rtd,dkc->rtkc', normed, w_qkv, preferred_element_type=jnp.flo...  3.58 us

profile of v1, /device:TPU:1, one launch (start us, length us, event | category | flops | bytes accessed | tf_op | source)
XLA Modules:
  0.0 95.2 jit_solution(13300022692211679103)
XLA Ops:
  0.0 0.7 add_convert_fusion.1
  0.7 0.1 copy.33
  0.8 1.3 %fusion.27 = f32[32,2]{1,0:T(8,128)S(1)} fusion(bf16[32,2,2048]{2,1,0:T(2,128)(2,1)} %param.9), kind=kLoop, calls=%fused_computation.26 | loop fusion | flops 393152 | bytes 262400 | tf_op jit(solution)/shard_map/reduce_sum | solution.py:463
  2.1 0.7 iota_compare_fusion
  2.8 0.8 copy.39
  3.6 0.5 multiply_cosine_fusion.1
  4.2 1.2 %fusion.28 = bf16[32,2,2048]{2,1,0:T(2,128)(2,1)S(1)} fusion(bf16[32,2,2048]{2,1,0:T(2,128)(2,1)} %param.9, f32[32,2]{1,0:T(8,128)S(1)} %add_rsqrt_fusion), kind=kLoop, calls=%fused_computation.27 | loop fusion | flops 393216 | bytes 524544 | tf_op jit(solution)/shard_map/convert_element_type | solution.py:464
  5.4 0.0 copy-start.2
  5.4 3.6 %fusion.8 = f32[32,2,1,1280]{3,0,1,2:T(8,128)S(1)} fusion(bf16[2048,1,1280]{2,0,1:T(8,128)(2,1)} %param.10, bf16[32,2,2048]{2,1,0:T(2,128)(2,1)S(1)} %fusion.28), kind=kOutput, calls=%fused_computation.8 | convolution fusion | flops 335544320 | bytes 5832704 | tf_op jit(solution)/shard_map/rtd,dkc->rtkc/dot_general | solution.py:32
  9.0 0.2 fusion.49
  9.3 0.1 maximum_bitcast_fusion
  9.4 0.1 reshape.225.hidden_ref
  9.5 0.1 fusion.52
  9.6 0.1 fusion.30
  9.7 0.8 fusion.54
  10.5 4.7 %fusion.53 = (f32[32,8,2]{1,2,0:T(2,128)S(1)}, f32[32,1,8,2,768]{4,2,3,0,1:T(8,128)S(1)}) fusion(bf16[32,1,2,768,128]{4,3,2,1,0:T(8,128)(2,1)} %param.12, bf16[32,2,8,64]{3,2,1,0:T(8,128)(2,1)S(1)} %get-tuple-element.6, bf16[32,2,8,64]{3,2,1,0:T(8,128)(2,1)S(1)} %get-tuple-element.5, pred[32,768]{1,0:T(8,128)(4,1)S(1)} %iota_compare_fusion), kind=kOutput, calls=%fused_computation.68 | convolution fusion | flops 102104576 | bytes 8022016 | tf_op jit(solution)/shard_map/rtkgh,rkch->rkgtc/dot_general | solution.py:46
  15.2 0.1 fusion.36
  15.3 0.4 fusion.14
  15.8 0.0 copy-start
  15.8 0.0 copy-start.1
  15.8 4.0 %fusion.16 = f32[32,128,8,2]{1,2,3,0:T(8,128)S(1)} fusion(bf16[32,1,2,768,128]{4,3,2,1,0:T(8,128)(2,1)} %param.12, f32[32,1,8,2,768]{4,2,3,0,1:T(8,128)S(1)} %get-tuple-element.14, f32[32,8,2]{1,2,0:T(2,128)S(1)} %max.9), kind=kOutput, calls=%fused_computation.14 | convolution fusion | flops 101449728 | bytes 8128512 | tf_op jit(solution)/shard_map/rkgtc,rkch->rtkgh/dot_general | solution.py:67
  19.8 0.3 fusion.23
  20.1 74.4 %shard_map.91 = bf16[64,512]{1,0:T(8,128)(2,1)S(1)} custom-call(bf16[64,1024]{1,0:T(8,128)(2,1)S(1)} %bitcast.100, bf16[64,2048]{1,0:T(8,128)(2,1)S(1)} %reshape.225.hidden_ref, bf16[2048,128]{1,0:T(8,128)(2,1)S(1)} %copy-done.1, s32[64,8]{1,0:T(8,128)S(1)} %bitcast.101, bf16[1024,2048]{1,0:T(8,128)(2,1)} %bitcast.103, bf16[2048,1536]{1,0:T(8,128)(2,1)} %bitcast.102, ...), custom_call_target="tpu_custom_call" | custom-call | tf_op jit(solution)/shard_map/pallas_call | solution.py:418
  94.5 0.7 reshape.227
  (12 shorter events, 0.2 us)
Async XLA Ops:
  5.4 4.0 %copy-start.2 = (bf16[32,2,2048]{2,1,0:T(2,128)(2,1)S(1)}, bf16[32,2,2048]{2,1,0:T(2,128)(2,1)}, u32[]{:S(2)}) copy-start(bf16[32,2,2048]{2,1,0:T(2,128)(2,1)} %param.9) | copy-start | bytes 786436
  15.8 4.3 %copy-start = (bf16[1,768,2048]{2,1,0:T(8,128)(2,1)S(1)}, bf16[1,768,2048]{2,1,0:T(8,128)(2,1)}, u32[]{:S(2)}) copy-start(bf16[1,768,2048]{2,1,0:T(8,128)(2,1)} %param.17) | copy-start | bytes 9437188
  15.8 4.3 %copy-start.1 = (bf16[2048,128]{1,0:T(8,128)(2,1)S(1)}, bf16[2048,128]{1,0:T(8,128)(2,1)}, u32[]{:S(2)}) copy-start(bf16[2048,128]{1,0:T(8,128)(2,1)} %router_ref.1) | copy-start | bytes 1572868

commit v2 on v1

--- a/solution.py
+++ b/solution.py
@@ -7,77 +7,6 @@
 
 ROPE_BASE = 1000000.0
 NORM_EPS = 1e-06
-
-
-def rotate_half(values, positions):
-    half_width = values.shape[-1] // 2
-    exponent = jnp.arange(half_width, dtype=jnp.float32) * (2.0 / values.shape[-1])
-    angles = positions * ROPE_BASE ** (-exponent)
-    cosine = jnp.cos(angles)
-    sine_part = jnp.sin(angles)
-    first_half = values[..., :half_width]
-    second_half = values[..., half_width:]
-    return jnp.concatenate(
-        [
-            first_half * cosine - second_half * sine_part,
-            second_half * cosine + first_half * sine_part,
-        ],
-        axis=-1,
-    )
-
-
-def attend(normed, w_qkv, cache_rows, length_rows):
-    head_dim = cache_rows.shape[-1]
-    group_size = w_qkv.shape[2] // head_dim - 2
-    projected = jnp.einsum("rtd,dkc->rtkc", normed, w_qkv, preferred_element_type=jnp.float32)
-    req_count, draft_len, kv_local, unused_width = projected.shape
-    positions = (length_rows[:, None] + jnp.arange(draft_len, dtype=jnp.int32)[None, :]).astype(
-        jnp.float32
-    )
-    query_part = projected[..., : group_size * head_dim].reshape(
-        req_count, draft_len, kv_local, group_size, head_dim
-    )
-    queries = rotate_half(query_part, positions[:, :, None, None, None]).astype(jnp.bfloat16)
-    key_part = projected[..., group_size * head_dim : (group_size + 1) * head_dim]
-    new_keys = rotate_half(key_part, positions[:, :, None, None]).astype(jnp.bfloat16)
-    new_values = projected[..., (group_size + 1) * head_dim :].astype(jnp.bfloat16)
-    score_scale = head_dim ** (-0.5)
-    old_scores = (
-        jnp.einsum(
-            "rtkgh,rkch->rkgtc", queries, cache_rows[:, :, 0], preferred_element_type=jnp.float32
-        )
-        * score_scale
-    )
-    fresh_scores = (
-        jnp.einsum("rtkgh,rskh->rkgts", queries, new_keys, preferred_element_type=jnp.float32)
-        * score_scale
-    )
-    context = cache_rows.shape[3]
-    old_live = jnp.arange(context, dtype=jnp.int32)[None, :] < length_rows[:, None]
-    fresh_live = (
-        jnp.arange(draft_len, dtype=jnp.int32)[None, :]
-        <= jnp.arange(draft_len, dtype=jnp.int32)[:, None]
-    )
-    old_scores = jnp.where(old_live[:, None, None, None, :], old_scores, -jnp.inf)
-    fresh_scores = jnp.where(fresh_live, fresh_scores, -jnp.inf)
-    row_top = jnp.maximum(jnp.max(old_scores, axis=-1), jnp.max(fresh_scores, axis=-1))[..., None]
-    old_exp = jnp.exp(old_scores - row_top)
-    fresh_exp = jnp.exp(fresh_scores - row_top)
-    totals = jnp.sum(old_exp, axis=-1) + jnp.sum(fresh_exp, axis=-1)
-    mixed_sum = jnp.einsum(
-        "rkgtc,rkch->rtkgh",
-        old_exp.astype(jnp.bfloat16),
-        cache_rows[:, :, 1],
-        preferred_element_type=jnp.float32,
-    )
-    mixed_sum = mixed_sum + jnp.einsum(
-        "rkgts,rskh->rtkgh",
-        fresh_exp.astype(jnp.bfloat16),
-        new_values,
-        preferred_element_type=jnp.float32,
-    )
-    head_out = (mixed_sum / jnp.transpose(totals, (0, 3, 1, 2))[..., None]).astype(jnp.bfloat16)
-    return head_out.reshape(req_count, draft_len, kv_local, group_size * head_dim)
 
 
 N_GROUPS = 4
@@ -87,8 +16,18 @@
 QUARTER = 512
 FF = 768
 EXPERTS = 128
+REQUESTS = 32
+HD = 128
+HEADS = 8
+CONTEXT = 768
+STEP = 4
 ROWS = 16 * N_MEMBERS
 PACKED = 1280
+FAR_FIRST = sorted(
+    range(1, N_MEMBERS),
+    key=lambda offset: -min(offset // 8, 4 - offset // 8)
+    - min(offset // 2 % 4, 4 - offset // 2 % 4),
+)
 F32 = jnp.float32
 BF16 = jnp.bfloat16
 
@@ -110,14 +49,22 @@
 
 
 def layer_kernel(
-    heads_ref,
+    lengths_ref,
+    speeds_ref,
     hidden_ref,
     router_ref,
     routes_ref,
+    w_qkv_hbm,
+    cache_hbm,
     w_out_hbm,
     gate_up_hbm,
     down_hbm,
     out_ref,
+    w_qkv,
+    cache,
+    queries,
+    fresh,
+    head_out,
     w_out,
     gate_up,
     down,
@@ -138,6 +85,8 @@
     made,
     moe_out,
     moe_in,
+    qkv_sem,
+    cache_sem,
     load_sem,
     rs_sem,
     ag_sem,
@@ -153,9 +102,39 @@
     def peer(offset):
         return lax.rem(group + offset, N_GROUPS)
 
+    x, z, core = member // 8, (member // 2) % 4, member % 2
+
     def other(offset):
-        return lax.rem(member + offset, N_MEMBERS)
-
+        return (
+            ((x + offset // 8) % 4) * 8
+            + ((z + (offset // 2) % 4) % 4) * 2
+            + (core + offset % 2) % 2
+        )
+
+    def source(offset):
+        return (
+            ((x + 4 - offset // 8) % 4) * 8
+            + ((z + 4 - (offset // 2) % 4) % 4) * 2
+            + (core + offset % 2) % 2
+        )
+
+    qkv_loads = [
+        pltpu.make_async_copy(
+            w_qkv_hbm.at[:, pl.ds(256 * chunk, 256)], w_qkv.at[chunk], qkv_sem.at[chunk]
+        )
+        for chunk in range(5)
+    ]
+    for load in qkv_loads:
+        load.start()
+
+    def cache_load(step):
+        block = pl.ds(step * STEP, STEP)
+        return pltpu.make_async_copy(
+            cache_hbm.at[block], cache.at[block], cache_sem.at[step]
+        )
+
+    for step in range(REQUESTS // STEP):
+        cache_load(step).start()
     order = (2, 1, 3, 0)
     loads = {}
     for offset in order:
@@ -187,7 +166,70 @@
             device_id_type=pl.DeviceIdType.MESH,
         )
 
-    heads = heads_ref[...]
+    row = iota((TOKENS, HD), 0)
+    places = (row % 2).astype(F32)
+    for request in range(REQUESTS):
+        length = lengths_ref[request].astype(F32)
+        places = places + jnp.where(row // 2 == request, length, 0.0)
+    angles = places * speeds_ref[...]
+    cosine = jnp.cos(angles)
+    sine = jnp.sin(angles)
+    sine = jnp.where(iota((TOKENS, HD), 1) < HD // 2, -sine, sine)
+
+    def rotate(values):
+        return (values * cosine + pltpu.roll(values, HD // 2, 1) * sine).astype(BF16)
+
+    tokens = hidden_ref[...].astype(F32)
+    scale = lax.rsqrt(jnp.mean(tokens * tokens, axis=-1, keepdims=True) + NORM_EPS)
+    normed = (tokens * scale).astype(BF16)
+
+    stacked = []
+    for chunk in range(4):
+        qkv_loads[chunk].wait()
+        projected = dot(normed, w_qkv[chunk])
+        stacked += [rotate(projected[:, :HD]), rotate(projected[:, HD:])]
+    row, col = iota((ROWS, ROWS), 0), iota((ROWS, ROWS), 1)
+    by_request = one_hot(((row // 2) % 8) * TOKENS + (row // 16) * 2 + row % 2 == col)
+    by_head = one_hot(((col // 2) % 8) * TOKENS + (col // 16) * 2 + col % 2 == row)
+    sorted_queries = dot(by_request, jnp.concatenate(stacked, axis=0)).astype(BF16)
+    queries[...] = sorted_queries.reshape(REQUESTS, 16, HD)
+    qkv_loads[4].wait()
+    projected = dot(normed, w_qkv[4])
+    new_keys = rotate(projected[:, :HD])
+    new_values = projected[:, HD:].astype(BF16)
+    row, col = iota((ROWS, TOKENS), 0), iota((ROWS, TOKENS), 1)
+    visible = (col // 2 == row // 16) & (col % 2 <= row % 2)
+    fresh_scores = dot_nt(sorted_queries, new_keys) * HD**-0.5
+    fresh[...] = jnp.where(visible, fresh_scores, -jnp.inf).reshape(REQUESTS, 16, TOKENS)
+
+    spot = iota((16, CONTEXT), 1)
+
+    @pl.loop(0, REQUESTS // STEP)
+    def _(step):
+        cache_load(step).wait()
+        for inner in range(STEP):
+            request = step * STEP + inner
+            scores = dot_nt(queries[request], cache[request, 0]) * HD**-0.5
+            scores = jnp.where(spot < lengths_ref[request], scores, -jnp.inf)
+            new_scores = fresh[request]
+            top = jnp.maximum(
+                jnp.max(scores, axis=-1, keepdims=True),
+                jnp.max(new_scores, axis=-1, keepdims=True),
+            )
+            old_exp = jnp.exp(scores - top)
+            new_exp = jnp.exp(new_scores - top)
+            totals = jnp.sum(old_exp, axis=-1, keepdims=True) + jnp.sum(
+                new_exp, axis=-1, keepdims=True
+            )
+            mixed = dot(old_exp.astype(BF16), cache[request, 1])
+            mixed = mixed + dot(new_exp.astype(BF16), new_values)
+            head_out[request] = (mixed / totals).astype(BF16)
+
+    by_heads = dot(by_head, head_out[...].reshape(ROWS, HD)).astype(BF16)
+    heads = jnp.concatenate(
+        [by_heads[TOKENS * head : TOKENS * head + TOKENS] for head in range(HEADS)], axis=1
+    )
+
     parts = {}
     for place, offset in enumerate(order):
         loads[offset].wait()
@@ -279,18 +321,16 @@
     def going(offset):
         return pltpu.make_async_remote_copy(
             src_ref=send.at[other(offset)],
-            dst_ref=recv.at[member],
+            dst_ref=recv.at[offset],
             send_sem=go_send.at[offset],
             recv_sem=go_recv.at[offset],
             device_id={"dev": other(offset)},
             device_id_type=pl.DeviceIdType.MESH,
         )
 
-    @pl.loop(1, N_MEMBERS)
-    def _(offset):
+    for offset in FAR_FIRST:
         going(offset).start()
-
-    recv[member] = send[member]
+    recv[0] = send[member]
 
     logits = dot(mid[...], router_ref[...])
     top = jnp.max(jnp.where(hit, logits, -jnp.inf), axis=-1, keepdims=True)
@@ -321,7 +361,7 @@
         going(offset).wait_send()
         pltpu.make_async_remote_copy(
             src_ref=send.at[other(offset)],
-            dst_ref=recv.at[other(N_MEMBERS - offset)],
+            dst_ref=recv.at[offset],
             send_sem=go_send.at[offset],
             recv_sem=go_recv.at[offset],
             device_id={"dev": other(offset)},
@@ -355,29 +395,27 @@
 
     def returning(offset):
         return pltpu.make_async_remote_copy(
-            src_ref=back.at[other(offset)],
+            src_ref=back.at[offset],
             dst_ref=home.at[member],
             send_sem=back_send.at[offset],
             recv_sem=back_recv.at[offset],
-            device_id={"dev": other(offset)},
-            device_id_type=pl.DeviceIdType.MESH,
-        )
-
-    @pl.loop(1, N_MEMBERS)
-    def _(offset):
+            device_id={"dev": source(offset)},
+            device_id_type=pl.DeviceIdType.MESH,
+        )
+
+    for offset in FAR_FIRST:
         returning(offset).start()
-
-    home[member] = back[member]
+    home[member] = back[0]
 
     @pl.loop(1, N_MEMBERS)
     def _(offset):
         returning(offset).wait_send()
         pltpu.make_async_remote_copy(
-            src_ref=back.at[other(offset)],
-            dst_ref=home.at[other(N_MEMBERS - offset)],
+            src_ref=back.at[offset],
+            dst_ref=home.at[other(offset)],
             send_sem=back_send.at[offset],
             recv_sem=back_recv.at[offset],
-            device_id={"dev": other(offset)},
+            device_id={"dev": source(offset)},
             device_id_type=pl.DeviceIdType.MESH,
         ).wait_recv()
 
@@ -409,7 +447,8 @@
     out_ref[...] = (resid[group].astype(F32) + moe).astype(BF16)
 
 
-def layer(heads, hidden, w_router, routes, w_out, gate_up, down):
+def layer(lengths, speeds, hidden, w_router, routes, w_qkv, cache, w_out, gate_up, down):
+    smem = pl.BlockSpec(memory_space=pltpu.SMEM)
     vmem = pl.BlockSpec(memory_space=pltpu.VMEM)
     hbm = pl.BlockSpec(memory_space=pl.ANY)
     dma = pltpu.SemaphoreType.DMA
@@ -418,9 +457,14 @@
     return pl.pallas_call(
         layer_kernel,
         out_shape=jax.ShapeDtypeStruct((TOKENS, QUARTER), BF16),
-        in_specs=[vmem] * 4 + [hbm] * 3,
+        in_specs=[smem] + [vmem] * 4 + [hbm] * 5,
         out_specs=vmem,
         scratch_shapes=[
+            pltpu.VMEM((5, WIDTH, 256), BF16),
+            pltpu.VMEM((REQUESTS, 2, CONTEXT, HD), BF16),
+            pltpu.VMEM((REQUESTS, 16, HD), BF16),
+            pltpu.VMEM((REQUESTS, 16, TOKENS), F32),
+            pltpu.VMEM((REQUESTS, 16, HD), BF16),
             pltpu.VMEM((N_GROUPS, 1024, QUARTER), BF16),
             pltpu.VMEM((WIDTH, 2 * FF), BF16),
             pltpu.VMEM((FF, WIDTH), BF16),
@@ -441,6 +485,8 @@
             pltpu.VMEM((ROWS, 256), BF16),
             parts,
             parts,
+            dma((5,)),
+            dma((REQUESTS // STEP,)),
             dma((6,)),
             dma((2, N_GROUPS)),
             dma((2, N_GROUPS)),
@@ -451,23 +497,23 @@
             dma((2, N_GROUPS)),
         ],
         compiler_params=pltpu.CompilerParams(
-            collective_id=0, has_side_effects=True, vmem_limit_bytes=48 * 1024 * 1024
+            collective_id=0, has_side_effects=True, vmem_limit_bytes=56 * 1024 * 1024
         ),
-    )(heads, hidden, w_router, routes, w_out, gate_up, down)
+    )(lengths, speeds, hidden, w_router, routes, w_qkv, cache, w_out, gate_up, down)
 
 
 def body(hidden_in, w_qkv, w_out, cache, lengths, w_router, routes, w_gate_up, w_down):
     req_count, draft_len, model_width = hidden_in.shape
-    token_f32 = hidden_in.astype(jnp.float32)
-    normed = (
-        token_f32 * lax.rsqrt(jnp.mean(token_f32 * token_f32, axis=-1, keepdims=True) + NORM_EPS)
-    ).astype(jnp.bfloat16)
-    head_out = attend(normed, w_qkv, cache, lengths)
+    exponent = jnp.arange(HD // 2, dtype=F32) * (2.0 / HD)
+    speeds = ROPE_BASE ** (-exponent)
     out = layer(
-        head_out.reshape(TOKENS, 1024),
+        lengths,
+        jnp.concatenate([speeds, speeds])[None, :],
         hidden_in.reshape(TOKENS, model_width),
         w_router,
         routes.reshape(TOKENS, 8),
+        w_qkv[:, 0],
+        cache[:, 0],
         w_out[0],
         w_gate_up[0],
         w_down[0],

time: 96.1 us -> 95.3 us (level)
  Pallas kernels: 74.4 us -> 88.8 us
  matrix products: 13.3 us -> 0 us
  other arithmetic: 5.47 us -> 0.68 us
  local copies, waits for them, and re-layouts: 1.87 us -> 4.63 us
    pallas_call x1, Pallas kernels: 74.4 us -> 88.8 us  [layer(): pl.pallas_call(layer_kernel, out_shape=jax.ShapeDtypeStruct((TOKENS, QUAR...]
    dot_general x5 -> x0, matrix products: 13.3 us -> none  [the longest x1 4.68 us: attend(): jnp.einsum('rtkgh,rkch->rkgtc', queries, cache_rows[:, :, 0], preferred_e...]
    convert_element_type x2 -> x0, other arithmetic: 1.89 us -> none  [the longest x1 1.22 us: body(): normed = (token_f32 * lax.rsqrt(jnp.mean(token_f32 * token_f32, axis=-1,...]
    reduce_sum x3 -> x0, other arithmetic: 1.88 us -> none  [the longest x1 1.3 us: body(): jnp.mean(token_f32 * token_f32, axis=-1, keepdims=True) + NORM_EPS]
    reshape x1, local copies, waits for them, and re-layouts: 0.1 us -> 1.74 us  [body(): hidden_in.reshape(TOKENS, model_width)]
where the time goes in v2:
time: 95.3 us; the launch traced here: 94.1 us
  Pallas kernels  88.8 us (93%)
  local copies, waits for them, and re-layouts  4.63 us (5%)
    pallas_call x1, Pallas kernels, layer(): pl.pallas_call(layer_kernel, out_shape=jax.ShapeDtypeStruct((TOKENS, QUAR...  88.8 us

profile of v2, /device:TPU:1, one launch (start us, length us, event | category | flops | bytes accessed | tf_op | source)
XLA Modules:
  0.0 94.1 jit_solution(2509429538648722786)
XLA Ops:
  0.0 0.7 maximum_bitcast_fusion.speeds_ref
  0.7 1.4 %copy.10 = s32[32,2,8]{2,1,0:T(2,128)} copy(s32[32,2,8]{0,2,1:T(8,128)} %param.15) | data formatting | bytes 4096 | tf_op args[6]
  2.1 1.7 %reshape.9.hidden_ref = bf16[64,2048]{1,0:T(8,128)(2,1)} reshape(bf16[32,2,2048]{2,1,0:T(2,128)(2,1)} %param.9) | data formatting | bytes 524288 | tf_op jit(solution)/shard_map/reshape | solution.py:512
  3.8 88.8 %shard_map.91 = bf16[64,512]{1,0:T(8,128)(2,1)} custom-call(s32[32]{0:T(128)} %lengths_ref.1, f32[1,128]{1,0:T(1,128)} %maximum_bitcast_fusion.speeds_ref, bf16[64,2048]{1,0:T(8,128)(2,1)} %reshape.9.hidden_ref, bf16[2048,128]{1,0:T(8,128)(2,1)} %router_ref.1, s32[64,8]{1,0:T(8,128)} %bitcast.13, bf16[2048,1280]{1,0:T(8,128)(2,1)} %bitcast.10, ...), custom_call_target="tpu_custom_call" | custom-call | tf_op jit(solution)/shard_map/pallas_call | solution.py:457
  92.6 1.5 %reshape.11 = bf16[32,2,512]{2,1,0:T(2,128)(2,1)} reshape(bf16[64,512]{1,0:T(8,128)(2,1)} %shard_map.91) | data formatting | bytes 131072 | tf_op jit(solution)/shard_map/reshape | solution.py:521
  (1 shorter events, 0.0 us)

commit v3 on v2

v3 whole, which is shorter than its diff:
```python
import jax
import jax.numpy as jnp
import numpy as np
from jax import lax
from jax.experimental import pallas as pl
from jax.experimental.pallas import tpu as pltpu
from jax.sharding import PartitionSpec as P

ROPE_BASE = 1000000.0
NORM_EPS = 1e-06
N_GROUPS = 4
N_MEMBERS = 32
TOKENS = 64
WIDTH = 2048
QUARTER = 512
FF = 768
EXPERTS = 128
REQUESTS = 32
HD = 128
HEADS = 8
CONTEXT = 768
BATCH = 8
ROWS = 16 * N_MEMBERS
PACKED = 640
MESH = pl.DeviceIdType.MESH
F32 = jnp.float32
BF16 = jnp.bfloat16


def iota(shape, axis):
    return lax.broadcasted_iota(jnp.int32, shape, axis)


def dot(a, b):
    return jnp.dot(a, b, preferred_element_type=F32)


def dot_nt(a, b):
    return lax.dot_general(a, b, (((1,), (1,)), ((), ())), preferred_element_type=F32)


def one_hot(mask):
    return jnp.where(mask, 1.0, 0.0).astype(BF16)


def layer_kernel(
    lengths_ref,
    speeds_ref,
    hidden_ref,
    router_ref,
    routes_ref,
    w_qkv_hbm,
    cache_hbm,
    w_out_hbm,
    gate_up_hbm,
    down_hbm,
    out_ref,
    w_qkv,
    cache,
    tokens,
    head_out,
    w_out,
    gate_up,
    down,
    part_out,
    part_in,
    resid,
    mid,
    sel_a,
    sel_b,
    comb_a,
    comb_b,
    send,
    relay,
    recv,
    back,
    back_relay,
    home,
    rows,
    inner_sums,
    acts,
    made,
    moe_out,
    moe_in,
    qkv_sem,
    cache_sem,
    load_sem,
    gate_sem,
    rs_sem,
    ag_sem,
    go_first,
    go_second,
    back_first,
    back_second,
    fin_sem,
):
    group = lax.axis_index("ga")
    member = lax.axis_index("dev")
    x, z, core = member // 8, (member // 2) % 4, member % 2

    def peer(offset):
        return lax.rem(group + offset, N_GROUPS)

    def other(offset):
        return (
            ((x + offset // 8) % 4) * 8
            + ((z + offset % 4) % 4) * 2
            + (core + (offset // 4) % 2) % 2
        )

    def mirror(offset):
        return (
            ((x + 4 - offset // 8) % 4) * 8
            + ((z + 4 - offset % 4) % 4) * 2
            + (core + (offset // 4) % 2) % 2
        )

    qkv_loads = [
        pltpu.make_async_copy(
            w_qkv_hbm.at[:, pl.ds(256 * chunk, 256)], w_qkv.at[chunk], qkv_sem.at[chunk]
        )
        for chunk in range(5)
    ]
    for load in qkv_loads:
        load.start()

    def cache_load(batch):
        block = pl.ds(batch * BATCH, BATCH)
        return pltpu.make_async_copy(
            cache_hbm.at[block], cache.at[block], cache_sem.at[batch]
        )

    cache_load(0).start()
    cache_load(1).start()
    order = (2, 1, 3, 0)
    loads = {}
    for offset in order:
        columns = pl.ds(pl.multiple_of(peer(offset) * QUARTER, QUARTER), QUARTER)
        loads[offset] = pltpu.make_async_copy(
            w_out_hbm.at[:, columns], w_out.at[offset], load_sem.at[offset]
        )
        loads[offset].start()
    cache_load(2).start()
    cache_load(3).start()
    load_gate_up = [
        pltpu.make_async_copy(
            gate_up_hbm.at[pl.ds(QUARTER * quarter + 256 * half, 256)],
            gate_up.at[half, pl.ds(256 * quarter, 256)],
            gate_sem.at[half, quarter],
        )
        for half in range(2)
        for quarter in range(N_GROUPS)
    ]
    for load in load_gate_up:
        load.start()
    load_down = pltpu.make_async_copy(down_hbm, down, load_sem.at[4])
    load_down.start()

    barrier = pltpu.get_barrier_semaphore()
    for offset in range(1, N_GROUPS):
        pl.semaphore_signal(
            barrier, inc=1, device_id={"ga": peer(offset)}, device_id_type=MESH
        )
    for offset in list(range(1, 8)) + [8, 16, 24]:
        pl.semaphore_signal(
            barrier, inc=1, device_id={"dev": other(offset)}, device_id_type=MESH
        )

    row = iota((TOKENS, HD), 0)
    places = (row % 2).astype(F32)
    for request in range(REQUESTS):
        length = lengths_ref[request].astype(F32)
        places = places + jnp.where(row // 2 == request, length, 0.0)
    angles = places * speeds_ref[...]
    cosine = jnp.cos(angles)
    sine = jnp.sin(angles)
    sine = jnp.where(iota((TOKENS, HD), 1) < HD // 2, -sine, sine)

    def rotate(values):
        return (values * cosine + pltpu.roll(values, HD // 2, 1) * sine).astype(BF16)

    hidden = hidden_ref[...].astype(F32).reshape(TOKENS, WIDTH)
    tokens[...] = hidden.astype(BF16)
    scale = lax.rsqrt(jnp.mean(hidden * hidden, axis=-1, keepdims=True) + NORM_EPS)
    normed = (hidden * scale).astype(BF16)

    stacked = []
    for chunk in range(4):
        qkv_loads[chunk].wait()
        projected = dot(normed, w_qkv[chunk])
        stacked += [rotate(projected[:, :HD]), rotate(projected[:, HD:])]
    row, col = iota((ROWS, ROWS), 0), iota((ROWS, ROWS), 1)
    by_request = one_hot(((row // 2) % 8) * TOKENS + (row // 16) * 2 + row % 2 == col)
    row, col = iota((256, 256), 0), iota((256, 256), 1)
    by_head = one_hot(((col // 2) % 8) * 32 + (col // 16) * 2 + col % 2 == row)
    queries = dot(by_request, jnp.concatenate(stacked, axis=0))
    qkv_loads[4].wait()
    projected = dot(normed, w_qkv[4])
    new_keys = rotate(projected[:, :HD])
    new_values = projected[:, HD:].astype(BF16)

    lane = iota((1, HD), 1)
    owner = iota((HD, HD), 1) // 16
    spot = iota((CONTEXT, HD), 0)
    row, col = iota((16, HD), 0), iota((16, HD), 1)
    visible = (row // 2 == col // 16) & (row % 2 <= col % 2)

    def score(batch):
        cache_load(batch).wait()
        first = batch * BATCH
        turned = queries[128 * batch : 128 * batch + 128].T
        blocks = [
            jnp.where(owner == inner, turned, 0.0).astype(BF16) for inner in range(BATCH)
        ]
        scores = dot(
            jnp.concatenate([cache[first + inner, 0] for inner in range(BATCH)], axis=1),
            jnp.concatenate(blocks, axis=0),
        )
        fresh = dot(new_keys[16 * batch : 16 * batch + 16], turned.astype(BF16))
        return scores, fresh

    def mix(batch, scores, fresh):
        first = batch * BATCH
        limits = jnp.zeros((1, HD), jnp.int32)
        for inner in range(BATCH):
            limits = jnp.where(lane // 16 == inner, lengths_ref[first + inner], limits)
        scores = jnp.where(spot < limits, scores * HD**-0.5, -jnp.inf)
        fresh = jnp.where(visible, fresh * HD**-0.5, -jnp.inf)
        top = jnp.maximum(
            jnp.max(scores, axis=0, keepdims=True), jnp.max(fresh, axis=0, keepdims=True)
        )
        old_exp = jnp.exp(scores - top)
        new_exp = jnp.exp(fresh - top)
        totals = jnp.sum(old_exp, axis=0, keepdims=True) + jnp.sum(
            new_exp, axis=0, keepdims=True
        )
        totals = jnp.broadcast_to(totals, (HD, HD)).T
        weights = old_exp.astype(BF16).T
        mixed = [
            dot(weights[16 * inner : 16 * inner + 16], cache[first + inner, 1])
            for inner in range(BATCH)
        ]
        mixed = jnp.concatenate(mixed, axis=0) + dot(
            new_exp.T.astype(BF16), new_values[16 * batch : 16 * batch + 16]
        )
        head_out[128 * batch : 128 * batch + 128] = (mixed / totals).astype(BF16)

    def part_copy(half, offset):
        return pltpu.make_async_remote_copy(
            src_ref=part_out.at[half, offset],
            dst_ref=part_in.at[half, offset],
            send_sem=rs_sem.at[0, half, offset],
            recv_sem=rs_sem.at[1, half, offset],
            device_id={"ga": peer(offset)},
            device_id_type=MESH,
        )

    def project(half):
        by_heads = dot(by_head, head_out[256 * half : 256 * half + 256]).astype(BF16)
        heads = jnp.concatenate(
            [by_heads[32 * head : 32 * head + 32] for head in range(HEADS)], axis=1
        )
        for place, offset in enumerate(order):
            if half == 0:
                loads[offset].wait()
            part_out[half, offset] = dot(heads, w_out[offset])
            if half == 0 and place == 0:
                pl.semaphore_wait(barrier, 13)
            if offset:
                part_copy(half, offset).start()

    def quarter_copy(half, offset, place):
        return pltpu.make_async_remote_copy(
            src_ref=resid.at[half, group],
            dst_ref=resid.at[half, place],
            send_sem=ag_sem.at[0, half, offset],
            recv_sem=ag_sem.at[1, half, offset],
            device_id={"ga": peer(offset)},
            device_id_type=MESH,
        )

    def residual(half):
        for offset in (1, 3, 2):
            part_copy(half, offset).wait()
        attn = part_out[half, 0] + part_in[half, 1] + part_in[half, 2] + part_in[half, 3]
        own = pl.ds(pl.multiple_of(group * QUARTER, QUARTER), QUARTER)
        held = tokens[32 * half : 32 * half + 32, own].astype(F32)
        resid[half, group] = (held + attn).astype(BF16)
        for offset in (2, 1, 3):
            quarter_copy(half, offset, group).start()

    pending = score(0)
    for batch in range(REQUESTS // BATCH):
        following = score(batch + 1) if batch < 3 else None
        mix(batch, *pending)
        pending = following
        if batch == 1:
            project(0)
    project(1)
    residual(0)

    hit = jnp.zeros((TOKENS, EXPERTS), F32)
    expert_of = iota((EXPERTS, REQUESTS), 0)
    row, col = iota((TOKENS, REQUESTS), 0), iota((TOKENS, REQUESTS), 1)
    for draft in range(2):
        named = routes_ref[draft, 0:1] == expert_of
        for choice in range(1, 8):
            named = named | (routes_ref[draft, choice : choice + 1] == expert_of)
        hit = hit + dot_nt(one_hot(row == 2 * col + draft), one_hot(named))
    hit = hit > 0.5
    earlier = one_hot(iota((TOKENS, TOKENS), 0) > iota((TOKENS, TOKENS), 1))
    slots = dot(earlier, one_hot(hit))
    code = jnp.where(hit, slots, -1.0).astype(BF16)
    code_a = jnp.concatenate([code] * 2, axis=0)
    code_b = jnp.concatenate([code] * 8, axis=0)
    base = group * N_MEMBERS
    spread = one_hot(
        other(iota((ROWS, EXPERTS), 0) // 16) + base == iota((ROWS, EXPERTS), 1)
    )
    row, col = iota((ROWS, 2 * TOKENS), 0), iota((ROWS, 2 * TOKENS), 1)
    sel_a[...] = one_hot(
        (dot_nt(spread, code_a) == (row % 8).astype(F32)) & ((row // 8) % 2 == col // TOKENS)
    )
    row, col = iota((ROWS, 8 * TOKENS), 0), iota((ROWS, 8 * TOKENS), 1)
    sel_b[...] = one_hot(
        (dot_nt(spread, code_b) == (8 + row % 2).astype(F32)) & ((row // 2) % 8 == col // TOKENS)
    )
    residual(1)
    for half in range(2):
        for offset in (1, 3, 2):
            quarter_copy(half, offset, group).wait_send()
            quarter_copy(half, offset, peer(N_GROUPS - offset)).wait_recv()
        here = slice(32 * half, 32 * half + 32)
        squares = jnp.zeros((32, 1), F32)
        for quarter in range(N_GROUPS):
            values = resid[half, quarter].astype(F32)
            squares = squares + jnp.sum(values * values, axis=-1, keepdims=True)
        scale = lax.rsqrt(squares / WIDTH + NORM_EPS)
        for quarter in range(N_GROUPS):
            mid[here, quarter * QUARTER : (quarter + 1) * QUARTER] = (
                resid[half, quarter].astype(F32) * scale
            ).astype(BF16)

    def exchange(half, outward, source, middle, final, first_sem, second_sem):
        at = other if outward else mirror
        source, middle, final = source.at[half], middle.at[half], final.at[half]

        def copy(src, dst, sem, index, offset):
            return pltpu.make_async_remote_copy(
                src_ref=src,
                dst_ref=dst,
                send_sem=sem.at[half, 0, index],
                recv_sem=sem.at[half, 1, index],
                device_id={"dev": at(offset)},
                device_id_type=MESH,
            )

        def along_x(dx):
            return copy(source.at[dx, 0], middle.at[dx, 0], first_sem, dx, 8 * dx)

        def along_z(dz):
            return copy(source.at[:, 1, dz], middle.at[:, 1, dz], first_sem, 4 + dz, 4 + dz)

        def then_z(dx, dz):
            origin = source if dx == 0 else middle
            return copy(origin.at[dx, 0, dz], final.at[dx, 0, dz], second_sem, 8 * dx + dz, dz)

        def then_x(dx, dz):
            origin, place = middle.at[dx, 1, dz], final.at[dx, 1, dz]
            return copy(origin, place, second_sem, 8 * dx + 4 + dz, 8 * dx)

        def start():
            for dx, dz in ((2, 2), (1, 1), (3, 3)):
                along_x(dx).start()
                along_z(dz).start()
            along_z(0).start()
            for dz in (2, 1, 3):
                then_z(0, dz).start()

        def forward():
            along_z(0).wait()
            for dx in (2, 1, 3):
                then_x(dx, 0).start()
            for dx, dz in ((1, 1), (3, 3), (2, 2)):
                along_x(dx).wait()
                for far in (2, 1, 3):
                    then_z(dx, far).start()
                along_z(dz).wait()
                for far in (2, 1, 3):
                    then_x(far, dz).start()
            final[0, 0, 0] = source[0, 0, 0]
            for place in range(1, 4):
                final[place, 0, 0] = middle[place, 0, 0]
            for place in range(4):
                final[0, 1, place] = middle[0, 1, place]

        def finish():
            for dx in range(4):
                for dz in range(4):
                    if dz:
                        then_z(dx, dz).wait()
                    if dx:
                        then_x(dx, dz).wait()

        return start, forward, finish

    going = []
    for half in range(2):
        pieces = [
            mid[:, quarter * QUARTER + 256 * half : quarter * QUARTER + 256 * half + 256]
            for quarter in range(N_GROUPS)
        ]
        wide = [jnp.concatenate(pieces[2 * k : 2 * k + 2], axis=1) for k in range(2)]
        packed = dot(sel_a[...], jnp.concatenate(wide, axis=0)).astype(BF16)
        send[half, :, :, :, :, :512] = packed.reshape(4, 2, 4, 16, 512)
        narrow = [pieces[k // 2][:, 128 * (k % 2) : 128 * (k % 2) + 128] for k in range(8)]
        packed = dot(sel_b[...], jnp.concatenate(narrow, axis=0)).astype(BF16)
        send[half, :, :, :, :, 512:] = packed.reshape(4, 2, 4, 16, 128)
        going.append(
            exchange(half, True, send, relay, recv, go_first, go_second)
        )
        going[half][0]()
    going[0][1]()
    going[1][1]()

    row, col = iota((ROWS, ROWS), 0), iota((ROWS, ROWS), 1)
    unpack = one_hot(((row % 64) // 2) * 16 + (row // 64) * 2 + row % 2 == col)
    pack = one_hot(((col % 64) // 2) * 16 + (col // 64) * 2 + col % 2 == row)

    for load in load_gate_up:
        load.wait()
    load_down.wait()

    for half in range(2):
        going[half][2]()
        got = recv[half, :, :, :, :, :512].reshape(N_MEMBERS, 16, 512).astype(F32)
        last = recv[half, :, :, :, :, 512:].reshape(ROWS, 128)
        last = dot(unpack, last).astype(BF16)
        for quarter in range(N_GROUPS):
            k, place = quarter // 2, 256 * (quarter % 2)
            start = 256 * quarter
            rows[:256, start : start + 256] = (
                got[:, 8 * k : 8 * k + 8, place : place + 256].reshape(256, 256).astype(BF16)
            )
            for j in range(2):
                at = 64 * (2 * quarter + j)
                rows[256:, start + 128 * j : start + 128 * j + 128] = last[at : at + 64]
        for chunk in range(6):
            columns = slice(256 * chunk, 256 * chunk + 256)
            product = dot(rows[...], gate_up[half, :, columns])
            if half == 0:
                inner_sums[:, columns] = product
            else:
                inner_sums[:, columns] += product
    gate = inner_sums[:, :FF]
    acts[...] = (gate / (1.0 + jnp.exp(-gate)) * inner_sums[:, FF:]).astype(BF16)
    coming = []
    for half in range(2):
        for quarter in range(N_GROUPS):
            k, place = quarter // 2, 256 * (quarter % 2)
            start = quarter * QUARTER + 256 * half
            result = dot(acts[...], down[:, start : start + 256])
            back[half, :, :, :, 8 * k : 8 * k + 8, place : place + 256] = (
                result[:256].astype(BF16).reshape(4, 2, 4, 8, 256)
            )
            for j in range(2):
                at = 64 * (2 * quarter + j)
                made[at : at + 64] = result[256:, 128 * j : 128 * j + 128].astype(BF16)
        back[half, :, :, :, :, 512:] = (
            dot(pack, made[...]).astype(BF16).reshape(4, 2, 4, 16, 128)
        )
        coming.append(
            exchange(half, False, back, back_relay, home, back_first, back_second)
        )
        coming[half][0]()
    gather = one_hot(
        other(iota((EXPERTS, ROWS), 1) // 16) + base == iota((EXPERTS, ROWS), 0)
    )
    row, col = iota((2 * TOKENS, ROWS), 0), iota((2 * TOKENS, ROWS), 1)
    mask_a = (dot(code_a, gather) == (col % 8).astype(F32)) & ((col // 8) % 2 == row // TOKENS)
    row, col = iota((8 * TOKENS, ROWS), 0), iota((8 * TOKENS, ROWS), 1)
    mask_b = (dot(code_b, gather) == (8 + col % 2).astype(F32)) & ((col // 2) % 8 == row // TOKENS)

    logits = dot(mid[...], router_ref[...])
    top = jnp.max(jnp.where(hit, logits, -jnp.inf), axis=-1, keepdims=True)
    raised = jnp.where(hit, jnp.exp(logits - top), 0.0)
    gates = raised / jnp.sum(raised, axis=-1, keepdims=True)
    rest = gates
    for term in range(3):
        piece = rest.astype(BF16)
        rest = rest - piece.astype(F32)
        spread_a = dot(jnp.concatenate([piece] * 2, axis=0), gather)
        comb = jnp.where(mask_a, spread_a, 0.0).astype(BF16)
        for k in range(2):
            comb_a[k, term * TOKENS : (term + 1) * TOKENS] = comb[k * TOKENS : (k + 1) * TOKENS]
        spread_b = dot(jnp.concatenate([piece] * 8, axis=0), gather)
        comb = jnp.where(mask_b, spread_b, 0.0).astype(BF16)
        for k in range(8):
            comb_b[k, term * TOKENS : (term + 1) * TOKENS] = comb[k * TOKENS : (k + 1) * TOKENS]
    coming[0][1]()
    coming[1][1]()

    def moe_copy(half, offset):
        return pltpu.make_async_remote_copy(
            src_ref=moe_out.at[half, offset],
            dst_ref=moe_in.at[half, offset],
            send_sem=fin_sem.at[0, half, offset],
            recv_sem=fin_sem.at[1, half, offset],
            device_id={"ga": peer(offset)},
            device_id_type=MESH,
        )

    for half in range(2):
        coming[half][2]()
        for offset in order:
            quarter = peer(offset)
            place = pl.ds(pl.multiple_of((quarter % 2) * 256, 256), 256)
            wide = home[half, :, :, :, :, place].reshape(ROWS, 256)
            summed = dot(comb_a[quarter // 2], wide)
            last = home[half, :, :, :, :, 512:].reshape(ROWS, 128)
            more = [dot(comb_b[2 * quarter + j], last) for j in range(2)]
            summed = summed + jnp.concatenate(more, axis=1)
            moe_out[half, offset] = (
                summed[:TOKENS] + summed[TOKENS : 2 * TOKENS] + summed[2 * TOKENS :]
            )
            if offset:
                moe_copy(half, offset).start()
    base = jnp.concatenate([resid[0, group], resid[1, group]], axis=0).astype(F32)
    for half in range(2):
        columns = slice(256 * half, 256 * half + 256)
        for offset in (1, 3, 2):
            moe_copy(half, offset).wait()
        moe = moe_out[half, 0] + moe_in[half, 1] + moe_in[half, 2] + moe_in[half, 3]
        final = base[:, columns] + moe
        out_ref[:, :, columns] = final.reshape(REQUESTS, 2, 256).astype(BF16)


def layer(lengths, hidden, w_router, routes, w_qkv, cache, w_out, gate_up, down):
    exponent = np.arange(HD // 2) * (2.0 / HD)
    speeds = np.tile(ROPE_BASE**-exponent, 2).astype(np.float32)[None, :]
    smem = pl.BlockSpec(memory_space=pltpu.SMEM)
    vmem = pl.BlockSpec(memory_space=pltpu.VMEM)
    hbm = pl.BlockSpec(memory_space=pl.ANY)
    dma = pltpu.SemaphoreType.DMA
    packed = pltpu.VMEM((2, 4, 2, 4, 16, PACKED), BF16)
    parts = pltpu.VMEM((2, N_GROUPS, 32, QUARTER), F32)
    sums = pltpu.VMEM((2, N_GROUPS, TOKENS, 256), F32)
    return pl.pallas_call(
        layer_kernel,
        out_shape=jax.ShapeDtypeStruct((REQUESTS, 2, QUARTER), BF16),
        in_specs=[smem] + [vmem] * 4 + [hbm] * 5,
        out_specs=vmem,
        scratch_shapes=[
            pltpu.VMEM((5, WIDTH, 256), BF16),
            pltpu.VMEM((REQUESTS, 2, CONTEXT, HD), BF16),
            pltpu.VMEM((TOKENS, WIDTH), BF16),
            pltpu.VMEM((ROWS, HD), BF16),
            pltpu.VMEM((N_GROUPS, 1024, QUARTER), BF16),
            pltpu.VMEM((2, WIDTH // 2, 2 * FF), BF16),
            pltpu.VMEM((FF, WIDTH), BF16),
            parts,
            parts,
            pltpu.VMEM((2, N_GROUPS, 32, QUARTER), BF16),
            pltpu.VMEM((TOKENS, WIDTH), BF16),
            pltpu.VMEM((ROWS, 2 * TOKENS), BF16),
            pltpu.VMEM((ROWS, 8 * TOKENS), BF16),
            pltpu.VMEM((2, 3 * TOKENS, ROWS), BF16),
            pltpu.VMEM((8, 3 * TOKENS, ROWS), BF16),
            packed,
            packed,
            packed,
            packed,
            packed,
            packed,
            pltpu.VMEM((320, WIDTH // 2), BF16),
            pltpu.VMEM((320, 2 * FF), F32),
            pltpu.VMEM((320, FF), BF16),
            pltpu.VMEM((ROWS, 128), BF16),
            sums,
            sums,
            dma((5,)),
            dma((REQUESTS // BATCH,)),
            dma((5,)),
            dma((2, N_GROUPS)),
            dma((2, 2, N_GROUPS)),
            dma((2, 2, N_GROUPS)),
            dma((2, 2, 8)),
            dma((2, 2, N_MEMBERS)),
            dma((2, 2, 8)),
            dma((2, 2, N_MEMBERS)),
            dma((2, 2, N_GROUPS)),
        ],
        compiler_params=pltpu.CompilerParams(
            collective_id=0, has_side_effects=True, vmem_limit_bytes=56 * 1024 * 1024
        ),
    )(lengths, speeds, hidden, w_router, routes, w_qkv, cache, w_out, gate_up, down)


def body(hidden_in, w_qkv, w_out, cache, lengths, w_router, routes, w_gate_up, w_down):
    return layer(
        lengths,
        hidden_in,
        w_router,
        jnp.transpose(routes, (1, 2, 0)),
        w_qkv[:, 0],
        cache[:, 0],
        w_out[0],
        w_gate_up[0],
        w_down[0],
    )


def solution(mesh):
    return jax.shard_map(
        body,
        mesh=mesh,
        in_specs=(
            P("dev", None, None),
            P(None, "ga", None),
            P("ga", None, None),
            P("dev", "ga", None, None, None),
            P("dev"),
            P(),
            P("dev", None, None),
            P(("ga", "dev"), None, None),
            P(("ga", "dev"), None, None),
        ),
        out_specs=P("dev", None, "ga"),
        check_vma=False,
    )
```

time: 95.3 us -> 78.5 us (0.82); the launches traced: 94.1 us -> 78.4 us
  Pallas kernels: 88.8 us -> 76.8 us
  local copies, waits for them, and re-layouts: 4.63 us -> 1.52 us
    pallas_call x1, Pallas kernels: 88.8 us -> 76.8 us  [layer(): pl.pallas_call(layer_kernel, out_shape=jax.ShapeDtypeStruct((REQUESTS, 2,...]
    reshape x2 -> x0, local copies, waits for them, and re-layouts: 3.24 us -> none  [the longest x1 1.74 us: body(): hidden_in.reshape(TOKENS, model_width)]
where the time goes in v3:
time: 78.5 us; the launch traced here: 78.4 us
  Pallas kernels  76.8 us (98%)
  local copies, waits for them, and re-layouts  1.52 us (2%)
    pallas_call x1, Pallas kernels, layer(): pl.pallas_call(layer_kernel, out_shape=jax.ShapeDtypeStruct((REQUESTS, 2,...  76.8 us

profile of v3, /device:TPU:1, one launch (start us, length us, event | category | flops | bytes accessed | tf_op | source)
XLA Modules:
  0.0 78.4 jit_solution(866607944913899916)
XLA Ops:
  0.0 76.8 %shard_map.100 = bf16[32,2,512]{2,1,0:T(2,128)(2,1)} custom-call(s32[32]{0:T(128)} %lengths_ref.1, f32[1,128]{1,0:T(1,128)} %constant.2.clone.speeds_ref, bf16[32,2,2048]{2,1,0:T(2,128)(2,1)} %hidden_ref.1, bf16[2048,128]{1,0:T(8,128)(2,1)} %router_ref.1, s32[2,8,32]{2,1,0:T(8,128)} %bitcast.11, bf16[2048,1280]{1,0:T(8,128)(2,1)} %bitcast.8, ...), custom_call_target="tpu_custom_call" | custom-call | tf_op jit(solution)/shard_map/pallas_call | solution.py:548
  76.9 1.5 %copy.12 = bf16[32,2,512]{2,1,0:T(2,128)(2,1)} copy(bf16[32,2,512]{2,1,0:T(2,128)(2,1)} %shard_map.100) | data formatting | bytes 131072

commit v4 on v3

--- a/solution.py
+++ b/solution.py
@@ -44,17 +44,20 @@
 
 
 def layer_kernel(
-    lengths_ref,
-    speeds_ref,
-    hidden_ref,
-    router_ref,
-    routes_ref,
+    lengths_hbm,
+    hidden_hbm,
+    router_hbm,
+    routes_hbm,
     w_qkv_hbm,
     cache_hbm,
     w_out_hbm,
     gate_up_hbm,
     down_hbm,
     out_ref,
+    lengths_ref,
+    hidden_ref,
+    router_ref,
+    routes_ref,
     w_qkv,
     cache,
     tokens,
@@ -82,6 +85,7 @@
     made,
     moe_out,
     moe_in,
+    small_sem,
     qkv_sem,
     cache_sem,
     load_sem,
@@ -115,6 +119,19 @@
             + (core + (offset // 4) % 2) % 2
         )
 
+    small_loads = [
+        pltpu.make_async_copy(source, target, small_sem.at[place])
+        for place, (source, target) in enumerate(
+            (
+                (hidden_hbm, hidden_ref),
+                (lengths_hbm, lengths_ref),
+                (routes_hbm, routes_ref),
+                (router_hbm, router_ref),
+            )
+        )
+    ]
+    for load in small_loads[:3]:
+        load.start()
     qkv_loads = [
         pltpu.make_async_copy(
             w_qkv_hbm.at[:, pl.ds(256 * chunk, 256)], w_qkv.at[chunk], qkv_sem.at[chunk]
@@ -142,6 +159,7 @@
         loads[offset].start()
     cache_load(2).start()
     cache_load(3).start()
+    small_loads[3].start()
     load_gate_up = [
         pltpu.make_async_copy(
             gate_up_hbm.at[pl.ds(QUARTER * quarter + 256 * half, 256)],
@@ -151,10 +169,7 @@
         for half in range(2)
         for quarter in range(N_GROUPS)
     ]
-    for load in load_gate_up:
-        load.start()
     load_down = pltpu.make_async_copy(down_hbm, down, load_sem.at[4])
-    load_down.start()
 
     barrier = pltpu.get_barrier_semaphore()
     for offset in range(1, N_GROUPS):
@@ -166,12 +181,19 @@
             barrier, inc=1, device_id={"dev": other(offset)}, device_id_type=MESH
         )
 
+    for load in small_loads[:3]:
+        load.wait()
     row = iota((TOKENS, HD), 0)
     places = (row % 2).astype(F32)
     for request in range(REQUESTS):
         length = lengths_ref[request].astype(F32)
         places = places + jnp.where(row // 2 == request, length, 0.0)
-    angles = places * speeds_ref[...]
+    speed_of = iota((1, HD), 1) % (HD // 2)
+    speeds = jnp.zeros((1, HD), F32)
+    for index in range(HD // 2):
+        speed = float(np.float32(ROPE_BASE ** (-2.0 * index / HD)))
+        speeds = jnp.where(speed_of == index, speed, speeds)
+    angles = places * speeds
     cosine = jnp.cos(angles)
     sine = jnp.sin(angles)
     sine = jnp.where(iota((TOKENS, HD), 1) < HD // 2, -sine, sine)
@@ -212,10 +234,17 @@
         blocks = [
             jnp.where(owner == inner, turned, 0.0).astype(BF16) for inner in range(BATCH)
         ]
-        scores = dot(
-            jnp.concatenate([cache[first + inner, 0] for inner in range(BATCH)], axis=1),
-            jnp.concatenate(blocks, axis=0),
-        )
+        wide = jnp.concatenate(blocks, axis=0)
+        scores = [
+            dot(
+                jnp.concatenate(
+                    [cache[first + inner, 0, part : part + 256] for inner in range(BATCH)], axis=1
+                ),
+                wide,
+            )
+            for part in range(0, CONTEXT, 256)
+        ]
+        scores = jnp.concatenate(scores, axis=0)
         fresh = dot(new_keys[16 * batch : 16 * batch + 16], turned.astype(BF16))
         return scores, fresh
 
@@ -296,6 +325,9 @@
         pending = following
         if batch == 1:
             project(0)
+    for load in load_gate_up:
+        load.start()
+    load_down.start()
     project(1)
     residual(0)
 
@@ -374,8 +406,6 @@
                 along_x(dx).start()
                 along_z(dz).start()
             along_z(0).start()
-            for dz in (2, 1, 3):
-                then_z(0, dz).start()
 
         def forward():
             along_z(0).wait()
@@ -388,6 +418,8 @@
                 along_z(dz).wait()
                 for far in (2, 1, 3):
                     then_x(far, dz).start()
+            for dz in (2, 1, 3):
+                then_z(0, dz).start()
             final[0, 0, 0] = source[0, 0, 0]
             for place in range(1, 4):
                 final[place, 0, 0] = middle[place, 0, 0]
@@ -481,6 +513,7 @@
     row, col = iota((8 * TOKENS, ROWS), 0), iota((8 * TOKENS, ROWS), 1)
     mask_b = (dot(code_b, gather) == (8 + col % 2).astype(F32)) & ((col // 2) % 8 == row // TOKENS)
 
+    small_loads[3].wait()
     logits = dot(mid[...], router_ref[...])
     top = jnp.max(jnp.where(hit, logits, -jnp.inf), axis=-1, keepdims=True)
     raised = jnp.where(hit, jnp.exp(logits - top), 0.0)
@@ -536,9 +569,6 @@
 
 
 def layer(lengths, hidden, w_router, routes, w_qkv, cache, w_out, gate_up, down):
-    exponent = np.arange(HD // 2) * (2.0 / HD)
-    speeds = np.tile(ROPE_BASE**-exponent, 2).astype(np.float32)[None, :]
-    smem = pl.BlockSpec(memory_space=pltpu.SMEM)
     vmem = pl.BlockSpec(memory_space=pltpu.VMEM)
     hbm = pl.BlockSpec(memory_space=pl.ANY)
     dma = pltpu.SemaphoreType.DMA
@@ -548,9 +578,13 @@
     return pl.pallas_call(
         layer_kernel,
         out_shape=jax.ShapeDtypeStruct((REQUESTS, 2, QUARTER), BF16),
-        in_specs=[smem] + [vmem] * 4 + [hbm] * 5,
+        in_specs=[hbm] * 9,
         out_specs=vmem,
         scratch_shapes=[
+            pltpu.SMEM((REQUESTS,), jnp.int32),
+            pltpu.VMEM((REQUESTS, 2, WIDTH), BF16),
+            pltpu.VMEM((WIDTH, EXPERTS), BF16),
+            pltpu.VMEM((2, 8, REQUESTS), jnp.int32),
             pltpu.VMEM((5, WIDTH, 256), BF16),
             pltpu.VMEM((REQUESTS, 2, CONTEXT, HD), BF16),
             pltpu.VMEM((TOKENS, WIDTH), BF16),
@@ -578,6 +612,7 @@
             pltpu.VMEM((ROWS, 128), BF16),
             sums,
             sums,
+            dma((4,)),
             dma((5,)),
             dma((REQUESTS // BATCH,)),
             dma((5,)),
@@ -593,7 +628,7 @@
         compiler_params=pltpu.CompilerParams(
             collective_id=0, has_side_effects=True, vmem_limit_bytes=56 * 1024 * 1024
         ),
-    )(lengths, speeds, hidden, w_router, routes, w_qkv, cache, w_out, gate_up, down)
+    )(lengths, hidden, w_router, routes, w_qkv, cache, w_out, gate_up, down)
 
 
 def body(hidden_in, w_qkv, w_out, cache, lengths, w_router, routes, w_gate_up, w_down):

time: 78.5 us -> 72.8 us (0.927)
  Pallas kernels: 76.8 us -> 70.4 us
    pallas_call x1, Pallas kernels: 76.8 us -> 70.4 us  [layer(): pl.pallas_call(layer_kernel, out_shape=jax.ShapeDtypeStruct((REQUESTS, 2,...]
where the time goes in v4:
time: 72.8 us; the launch traced here: 71.9 us
  Pallas kernels  70.4 us (97%)
  local copies, waits for them, and re-layouts  1.52 us (2%)
    pallas_call x1, Pallas kernels, layer(): pl.pallas_call(layer_kernel, out_shape=jax.ShapeDtypeStruct((REQUESTS, 2,...  70.4 us
    unnamed x1, local copies, waits for them, and re-layouts  1.52 us

profile of v4, /device:TPU:1, one launch (start us, length us, event | category | flops | bytes accessed | tf_op | source)
XLA Modules:
  0.0 71.9 jit_solution(758011302187994936)
XLA Ops:
  0.0 70.4 %shard_map.91 = bf16[32,2,512]{2,1,0:T(2,128)(2,1)} custom-call(s32[32]{0:T(128)} %lengths_hbm.1, bf16[32,2,2048]{2,1,0:T(2,128)(2,1)} %hidden_hbm.1, bf16[2048,128]{1,0:T(8,128)(2,1)} %router_hbm.1, s32[2,8,32]{2,1,0:T(8,128)} %bitcast.11, bf16[2048,1280]{1,0:T(8,128)(2,1)} %bitcast.8, bf16[32,2,768,128]{3,2,1,0:T(8,128)(2,1)} %bitcast.6, ...), custom_call_target="tpu_custom_call" | custom-call | tf_op jit(solution)/shard_map/pallas_call | solution.py:578
  70.4 1.5 %copy.11 = bf16[32,2,512]{2,1,0:T(2,128)(2,1)} copy(bf16[32,2,512]{2,1,0:T(2,128)(2,1)} %shard_map.91) | data formatting | bytes 131072

commit v5 on v4

--- a/solution.py
+++ b/solution.py
@@ -412,14 +412,15 @@
             for dx in (2, 1, 3):
                 then_x(dx, 0).start()
             for dx, dz in ((1, 1), (3, 3), (2, 2)):
+                if dx == 2:
+                    for near in (2, 1, 3):
+                        then_z(0, near).start()
                 along_x(dx).wait()
                 for far in (2, 1, 3):
                     then_z(dx, far).start()
                 along_z(dz).wait()
                 for far in (2, 1, 3):
                     then_x(far, dz).start()
-            for dz in (2, 1, 3):
-                then_z(0, dz).start()
             final[0, 0, 0] = source[0, 0, 0]
             for place in range(1, 4):
                 final[place, 0, 0] = middle[place, 0, 0]

time: 72.8 us -> 72.7 us (level)
  no operation moved by 1% of the time
where the time goes in v5:
time: 72.7 us; the launch traced here: 71.9 us
  Pallas kernels  70.4 us (97%)
  local copies, waits for them, and re-layouts  1.52 us (2%)
    pallas_call x1, Pallas kernels, layer(): pl.pallas_call(layer_kernel, out_shape=jax.ShapeDtypeStruct((REQUESTS, 2,...  70.4 us
    unnamed x1, local copies, waits for them, and re-layouts  1.52 us

profile of v5, /device:TPU:1, one launch (start us, length us, event | category | flops | bytes accessed | tf_op | source)
XLA Modules:
  0.0 71.9 jit_solution(8608967243242202858)
XLA Ops:
  0.0 70.4 %shard_map.91 = bf16[32,2,512]{2,1,0:T(2,128)(2,1)} custom-call(s32[32]{0:T(128)} %lengths_hbm.1, bf16[32,2,2048]{2,1,0:T(2,128)(2,1)} %hidden_hbm.1, bf16[2048,128]{1,0:T(8,128)(2,1)} %router_hbm.1, s32[2,8,32]{2,1,0:T(8,128)} %bitcast.11, bf16[2048,1280]{1,0:T(8,128)(2,1)} %bitcast.8, bf16[32,2,768,128]{3,2,1,0:T(8,128)(2,1)} %bitcast.6, ...), custom_call_target="tpu_custom_call" | custom-call | tf_op jit(solution)/shard_map/pallas_call | solution.py:579
  70.4 1.5 %copy.11 = bf16[32,2,512]{2,1,0:T(2,128)(2,1)} copy(bf16[32,2,512]{2,1,0:T(2,128)(2,1)} %shard_map.91) | data formatting | bytes 131072
